TPU v7x, 512 devices: a whole 4x8x8 slice. The times are simulated.
512 devices in a mesh: dp: 64 (over y, z), mp: 8 (over x, core).
Axes of the slice: x: 4, y: 8, z: 8, core: 2. Of those that a mesh axis runs over, the one named last changes fastest.
Arguments:
- context: bfloat16 [12288, 2048], P('dp', 'mp'), may hold values from -8 to 8, as said below
- cotangent: bfloat16 [12288, 4096], P('dp'), may hold values from -8 to 8, as said below
- master_weight: float32 [2048, 4096], P(('mp', 'dp')), may hold values from -0.09375 to 0.09375
- row_state: float32 [2048], P(('mp', 'dp')), may hold values from 0.1 to 1
- col_state: float32 [4096], replicated, may hold values from 0.16666667 to 1.6666666
Outputs:
- grad_input: bfloat16 [12288, 2048], P('dp', 'mp')
- update: float32 [2048, 4096], P(('mp', 'dp'))
- row_new: float32 [2048], P(('mp', 'dp'))
- col_new: float32 [4096], replicated
- update_rms: float32 [], replicated
Inputs may be any that keep to these rules, and one draw needn't show every extreme that they name: context values, column scales vary. cotangent values, column scales vary.
All inputs are finite; a program needn't handle non-finite values.
Results may differ from a plain program's by a relative error of at most 0.001.
The roundings to bfloat16 on the way count: a program that leaves them out, or rounds other values in their place, can miss the bound.
Values may be sent and summed in bfloat16 or wider, within the bound.
No kernel may reach another device: no remote copies, remote signals or barrier semaphores. Data moves between devices by JAX's collectives and lax.ppermute only.
A program may use at most 64 MiB of HBM per device.

v0:
```python
import jax
import jax.numpy as jnp
from jax import lax
from jax.sharding import PartitionSpec as P

BETA = 0.8
EPS1 = 1e-30
CLIP = 1.0


def on_device(context, cotangent, master_weight, row_state, col_state):
    tok_dev = cotangent.shape[0]
    inv_tokens = 1.0 / (tok_dev * lax.axis_size("dp"))
    local_rows = master_weight.shape[0]
    weight_copy = master_weight.astype(jnp.bfloat16)
    grad_input = lax.dot_general(
        cotangent,
        lax.all_gather(weight_copy, "dp", axis=0, tiled=True),
        (((1,), (1,)), ((), ())),
        preferred_element_type=jnp.float32,
    ).astype(jnp.bfloat16)
    term = (
        lax.dot_general(
            context, cotangent, (((0,), (0,)), ((), ())), preferred_element_type=jnp.float32
        )
        * inv_tokens
    )
    grad = lax.psum_scatter(term, "dp", scatter_dimension=0, tiled=True)
    squared = grad * grad + EPS1
    row_new = BETA * row_state + (1.0 - BETA) * jnp.sum(squared, axis=1)
    col_part = jnp.sum(squared, axis=0)
    entries = local_rows * lax.axis_size("dp") * lax.axis_size("mp") * grad.shape[1]
    col_total, row_total = lax.psum((col_part, jnp.sum(row_new)), ("dp", "mp"))
    col_new = BETA * col_state + (1.0 - BETA) * col_total
    scaled = grad / jnp.sqrt(row_new[:, None] * col_new[None, :] / row_total)
    square_sum = lax.psum(jnp.sum(scaled * scaled), ("dp", "mp"))
    update_rms = jnp.sqrt(square_sum / entries)
    update = scaled / jnp.maximum(CLIP, update_rms)
    return (grad_input, update, row_new, col_new, update_rms)


def solution(mesh):
    in_specs = (P("dp", "mp"), P("dp", None), P(("mp", "dp"), None), P(("mp", "dp")), P())
    out_specs = (P("dp", "mp"), P(("mp", "dp"), None), P(("mp", "dp")), P(), P())
    return jax.shard_map(
        on_device, mesh=mesh, in_specs=in_specs, out_specs=out_specs, check_vma=False
    )
```

profile of v0, /device:TPU:1, one launch (start us, length us, event | category | flops | bytes accessed | tf_op | source)
XLA Modules:
  0.0 474.0 jit_solution(12807350279696116664)
XLA Ops:
  7.2 0.0 copy-start
  7.2 0.0 all-gather.3.cloned.1.call-start
  7.2 1.6 convert_bitcast_fusion
  8.8 0.0 all-gather.3.cloned.1.call-update
  8.8 0.0 all-reduce.4.cloned.1.call-start
  8.9 0.0 copy-done
  8.9 3.6 convolution_multiply_fusion
  12.5 0.0 all-reduce.4.cloned.1.call-update
  12.5 1.3 dynamic-slice
  14.4 82.5 %all-gather.3.cloned.1.call-done = bf16[64,4,4096]{2,1,0:T(4,128)(2,1)} async-done(((bf16[1,4,4096]{2,1,0:T(4,128)(2,1)}), bf16[64,4,4096]{2,1,0:T(4,128)(2,1)}) %all-gather.3.cloned.1.call-update) | async-done | bytes 2097168 | tf_op jit(solution)/shard_map/all_gather | solution.py:18
  96.9 4.0 reshape.13
  100.9 0.0 copy-start.4
  100.9 0.0 copy-start.2
  100.9 3.1 convolution_convert_fusion
  104.0 163.8 %all-reduce.4.cloned.1.call-done = f32[256,4096]{1,0:T(8,128)} async-done(((f32[256,4096]{1,0:T(8,128)}), f32[256,4096]{1,0:T(8,128)}) %all-reduce.4.cloned.1.call-update) | async-done | bytes 4194320
  267.8 1.1 fusion
  268.9 0.0 copy-done.4
  268.9 0.6 fusion.2
  269.5 0.0 copy-start.3
  269.5 98.9 %all-reduce.1 = (f32[]{:T(128)}, f32[4096]{0:T(1024)S(1)}) all-reduce(f32[]{:T(128)} %get-tuple-element.11, f32[4096]{0:T(1024)S(1)} %get-tuple-element.5), channel_id=1, replica_groups=mesh['dp'=64,'mp'=8] {'dp','mp'}, use_global_device_ids=true, to_apply=%region_5.0 | all-reduce | flops 4097 | bytes 32776 | tf_op jit(solution)/shard_map/psum | solution.py:33
  368.4 0.0 copy-done.2
  368.4 0.0 copy-start.1
  368.4 2.3 multiply_reduce_fusion
  370.7 94.0 %psum.23 = f32[]{:T(128)} all-reduce(f32[]{:T(128)} %get-tuple-element.9), channel_id=1, replica_groups=mesh['dp'=64,'mp'=8] {'dp','mp'}, use_global_device_ids=true, to_apply=%region_7.0 | all-reduce | flops 1 | bytes 8 | tf_op jit(solution)/shard_map/psum | solution.py:36
  465.4 0.6 broadcast_divide_fusion
  466.0 0.0 copy-done.3
  466.0 0.0 copy-done.1
  (1 shorter events, 0.0 us)
Async XLA Ops:
  7.2 1.7 copy-start
  7.2 89.8 %all-gather.3.cloned.1.call-start = ((), (), s32[]{:S(2)}) async-start(), calls=%async_computation | async-start | bytes 2129920 | tf_op jit(solution)/shard_map/all_gather | solution.py:18
  8.8 259.0 %all-reduce.4.cloned.1.call-start = ((), (), s32[]{:S(2)}) async-start(), calls=%async_computation.1 | async-start | bytes 8388608
  100.9 167.9 %copy-start.4 = (f32[4]{0:T(128)S(1)}, f32[4]{0:T(128)}, u32[]{:S(2)}) copy-start(f32[4]{0:T(128)} %param.8) | copy-start | bytes 52
  100.9 267.5 %copy-start.2 = (f32[4096]{0:T(1024)S(1)}, f32[4096]{0:T(1024)}, u32[]{:S(2)}) copy-start(f32[4096]{0:T(1024)} %param.9) | copy-start | bytes 49156
  269.5 196.5 %copy-start.3 = (f32[4]{0:T(128)}, f32[4]{0:T(128)S(1)}, u32[]{:S(2)}) copy-start(f32[4]{0:T(128)S(1)} %get-tuple-element.12) | copy-start | bytes 52
  368.4 97.6 %copy-start.1 = (f32[4096]{0:T(1024)}, f32[4096]{0:T(1024)S(1)}, u32[]{:S(2)}) copy-start(f32[4096]{0:T(1024)S(1)} %multiply_add_fusion.1) | copy-start | bytes 49156
Sparse Core Ops, SparseCore 0:
  11.6 85.2 all-gather.2
  100.2 167.5 all-reduce.3
where the time goes:
time: 475 us; the launch traced here: 474 us
  waiting for transfers between devices  246 us (52%)
  blocking collectives  193 us (41%)
  between operations  16.6 us (3%)
  matrix products  6.7 us (1%)
  other arithmetic  6.17 us (1%)
  local copies, waits for them, and re-layouts  5.29 us (1%)
    unnamed x3, waiting for transfers between devices  164 us
    psum x1, blocking collectives, on_device(): col_total, row_total = lax.psum((col_part, jnp.sum(row_new)), ('dp', 'mp'))  98.9 us
    psum x1, blocking collectives, on_device(): square_sum = lax.psum(jnp.sum(scaled * scaled), ('dp', 'mp'))  94 us
    all_gather x1, waiting for transfers between devices, on_device(): lax.all_gather(weight_copy, 'dp', axis=0, tiled=True)  82.5 us
  transfers between devices with their start and end apart: 2, of which 2 were waited for; matrix products, arithmetic and copies ran while one was open for 3% of the time, Pallas kernels for 0%

commit v1 on v0

v1 whole, which is shorter than its diff:
```python
import jax
import jax.numpy as jnp
from jax import lax
from jax.sharding import Mesh, PartitionSpec as P

BETA = 0.8
EPS1 = 1e-30
CLIP = 1.0
OTHER = ("z", "x", "c")


def spread(value, axes, size):
    copies = jnp.broadcast_to(value[None], (size,) + value.shape)
    return lax.all_to_all(copies, axes, 0, 0, tiled=True)


def on_device(context, cotangent, master_weight, row_state, col_state):
    ny, nz = lax.axis_size("y"), lax.axis_size("z")
    nmp = lax.axis_size("x") * lax.axis_size("c")
    n_other = nz * nmp
    rows, cols = master_weight.shape
    inv_tokens = 1.0 / (cotangent.shape[0] * ny * nz)
    entries = rows * ny * nz * nmp * cols

    term = (
        lax.dot_general(
            context, cotangent, (((0,), (0,)), ((), ())), preferred_element_type=jnp.float32
        )
        * inv_tokens
    )
    part = lax.psum_scatter(term, "y", scatter_dimension=0, tiled=True)

    weight_copy, _ = lax.optimization_barrier((master_weight.astype(jnp.bfloat16), term))
    weight_rows = spread(weight_copy, "z", nz).reshape(nz * rows, cols)
    weight_rows, part = lax.optimization_barrier((weight_rows, part))
    weight = lax.all_gather(weight_rows, "y", axis=0, tiled=True)
    grad_input = lax.dot_general(
        cotangent, weight, (((1,), (1,)), ((), ())), preferred_element_type=jnp.float32
    ).astype(jnp.bfloat16)

    grad = jnp.sum(
        lax.all_to_all(part.reshape(nz, rows, cols), "z", 0, 0, tiled=True), axis=0
    )
    squared = grad * grad + EPS1
    row_new = BETA * row_state + (1.0 - BETA) * jnp.sum(squared, axis=1)
    col_part = jnp.sum(squared, axis=0)
    ratio_part = jnp.sum(grad * grad / row_new[:, None], axis=0)
    lanes = 2 * cols // n_other
    sums = jnp.concatenate([col_part, ratio_part]).reshape(n_other, 1, lanes)
    extra = jnp.broadcast_to(jnp.sum(row_new), (n_other, 1, lanes))
    packed = jnp.concatenate([sums, extra], axis=1)
    packed = jnp.sum(lax.all_to_all(packed, OTHER, 0, 0, tiled=True), axis=0)
    packed = jnp.sum(spread(packed, "y", ny), axis=0)
    packed = spread(packed, OTHER, n_other)
    both = packed[:, 0].reshape(2, cols)
    row_total = packed[0, 1, 0]
    col_new = BETA * col_state + (1.0 - BETA) * both[0]
    update_rms = jnp.sqrt(row_total * jnp.sum(both[1] / col_new) / entries)
    scaled = grad / jnp.sqrt(row_new[:, None] * col_new[None, :] / row_total)
    update = scaled / jnp.maximum(CLIP, update_rms)
    return (grad_input, update, row_new, col_new, update_rms)


def solution(mesh):
    grid = Mesh(mesh.devices.reshape(8, 8, 4, 2), ("y", "z", "x", "c"))
    dp, mp = ("y", "z"), ("x", "c")
    in_specs = (P(dp, mp), P(dp, None), P(mp + dp, None), P(mp + dp), P())
    out_specs = (P(dp, mp), P(mp + dp, None), P(mp + dp), P(), P())
    return jax.shard_map(
        on_device, mesh=grid, in_specs=in_specs, out_specs=out_specs, check_vma=False
    )
```

time: 475 us -> 160 us (0.34)
  waiting for transfers between devices: 246 us -> 40.6 us
  blocking collectives: 193 us -> 86.8 us
    psum x2 -> x0, blocking collectives: 193 us -> none  [the longest x1 98.9 us: on_device(): col_total, row_total = lax.psum((col_part, jnp.sum(row_new)), ('dp', 'mp'))]
    unnamed x3 -> x2, waiting for transfers between devices: 164 us -> 0.03 us
    all_to_all x0 -> x5, blocking collectives: none -> 86.8 us  [the longest x3 46.8 us: spread(): return lax.all_to_all(copies, axes, 0, 0, tiled=True)]
    all_gather x1, waiting for transfers between devices: 82.5 us -> 0.01 us  [on_device(): weight = lax.all_gather(weight_rows, 'y', axis=0, tiled=True)]
    reduce_scatter x0 -> x1, waiting for transfers between devices: none -> 40.6 us  [on_device(): part = lax.psum_scatter(term, 'y', scatter_dimension=0, tiled=True)]
  transfers between devices with their start and end apart: 2 -> 2, of which waited for: 2 -> 1; matrix products, arithmetic and copies ran while one was open for 3% -> 4% of each run, Pallas kernels for 0% -> 0%
where the time goes in v1:
time: 160 us; the launch traced here: 159 us
  blocking collectives  86.8 us (54%)
  waiting for transfers between devices  40.6 us (25%)
  between operations  16.6 us (10%)
  matrix products  6.64 us (4%)
  local copies, waits for them, and re-layouts  4.72 us (3%)
  other arithmetic  3.75 us (2%)
    all_to_all x3, blocking collectives, spread(): return lax.all_to_all(copies, axes, 0, 0, tiled=True)  46.8 us
    reduce_scatter x1, waiting for transfers between devices, on_device(): part = lax.psum_scatter(term, 'y', scatter_dimension=0, tiled=True)  40.6 us
    all_to_all x1, blocking collectives, on_device(): lax.all_to_all(part.reshape(nz, rows, cols), 'z', 0, 0, tiled=True)  23 us
    all_to_all x1, blocking collectives, on_device(): packed = jnp.sum(lax.all_to_all(packed, OTHER, 0, 0, tiled=True), axis=0)  17 us
    dot_general x1, matrix products, on_device(): lax.dot_general(context, cotangent, (((0,), (0,)), ((), ())), preferred_e...  3.55 us
  transfers between devices with their start and end apart: 2, of which 1 were waited for; matrix products, arithmetic and copies ran while one was open for 4% of the time, Pallas kernels for 0%

profile of v1, /device:TPU:1, one launch (start us, length us, event | category | flops | bytes accessed | tf_op | source)
XLA Modules:
  0.0 159.2 jit_solution(389512499405463202)
XLA Ops:
  7.2 0.0 copy-start
  7.2 0.0 reduce-scatter.2.cloned.1.call-start
  7.2 1.4 copy-done
  8.6 3.6 %convolution_multiply_fusion = f32[256,4096]{1,0:T(8,128)} fusion(bf16[192,256]{1,0:T(8,128)(2,1)} %param.5, bf16[192,4096]{1,0:T(8,128)(2,1)S(1)} %copy-done), kind=kOutput, calls=%fused_computation | convolution fusion | flops 403701760 | bytes 5865472 | tf_op jit(solution)/shard_map/dot_general | solution.py:26
  12.1 0.0 reduce-scatter.2.cloned.1.call-update
  12.2 0.0 all-gather.2.cloned.1.call-start
  12.2 0.8 copy-done.1
  13.0 0.1 broadcast_in_dim.6
  13.1 0.0 copy-start.5
  13.1 21.0 %all_to_all.25 = bf16[8,4,4096]{2,1,0:T(4,128)(2,1)S(1)} all-to-all(bf16[8,4,4096]{2,1,0:T(4,128)(2,1)S(1)} %broadcast_in_dim.6), channel_id=1, replica_groups=mesh['y'=8,'z'=8,'x'=4,'c'=2] {'z'}, dimensions={0} | all-to-all | bytes 524288 | tf_op jit(solution)/shard_map/all_to_all | solution.py:14
  34.1 0.8 reshape.30
  34.9 40.6 %reduce-scatter.2.cloned.1.call-done = f32[32,4096]{1,0:T(8,128)} async-done(((f32[256,4096]{1,0:T(8,128)}), f32[32,4096]{1,0:T(8,128)}) %reduce-scatter.2.cloned.1.call-update) | async-done | bytes 524304 | tf_op jit(solution)/shard_map/reduce_scatter | solution.py:31
  75.5 0.0 all-gather.2.cloned.1.call-update
  75.5 1.2 reshape.31
  76.7 23.0 %all_to_all.26 = f32[8,4,4096]{2,1,0:T(4,128)S(1)} all-to-all(f32[8,4,4096]{2,1,0:T(4,128)S(1)} %reshape.31), channel_id=1, replica_groups=mesh['y'=8,'z'=8,'x'=4,'c'=2] {'z'}, dimensions={0} | all-to-all | bytes 1048576 | tf_op jit(solution)/shard_map/all_to_all | solution.py:42
  99.7 0.1 reduce_sum.72
  99.8 0.1 add_reduce_fusion.1
  99.9 0.0 copy-done.5
  99.9 0.6 fusion.1
  100.5 0.1 add_reduce_fusion
  100.6 0.7 select_maximum_fusion
  101.3 17.0 %all_to_all.27 = f32[64,2,128]{2,1,0:T(2,128)S(1)} all-to-all(f32[64,2,128]{2,1,0:T(2,128)S(1)} %select_maximum_fusion), channel_id=1, replica_groups=mesh['y'=8,'z'=8,'x'=4,'c'=2] {'z','x','c'}, dimensions={0} | all-to-all | bytes 131072 | tf_op jit(solution)/shard_map/all_to_all | solution.py:52
  118.4 0.1 reduce_sum.77
  118.5 10.6 %all_to_all.28 = f32[8,2,128]{2,1,0:T(2,128)S(1)} all-to-all(f32[8,2,128]{2,1,0:T(2,128)S(1)} %broadcast_in_dim.7), channel_id=1, replica_groups=mesh['y'=8,'z'=8,'x'=4,'c'=2] {'y'}, dimensions={0} | all-to-all | bytes 16384 | tf_op jit(solution)/shard_map/all_to_all | solution.py:14
  129.1 15.2 %all_to_all.29 = f32[64,2,128]{2,1,0:T(2,128)S(1)} all-to-all(f32[64,2,128]{2,1,0:T(2,128)S(1)} %broadcast_in_dim.8), channel_id=1, replica_groups=mesh['y'=8,'z'=8,'x'=4,'c'=2] {'z','x','c'}, dimensions={0} | all-to-all | bytes 131072 | tf_op jit(solution)/shard_map/all_to_all | solution.py:14
  144.3 0.5 slice.18
  144.8 0.0 copy-done.3
  144.8 0.6 divide_reduce_fusion.1
  146.8 1.4 multiply_divide_fusion
  148.2 3.1 %fusion = bf16[192,256]{1,0:T(8,128)(2,1)} fusion(bf16[256,4096]{1,0:T(8,128)(2,1)} %all-gather.2.cloned.1.call-done, bf16[192,4096]{1,0:T(8,128)(2,1)S(1)} %copy-done), kind=kOutput, calls=%fused_computation.2 | convolution fusion | flops 402702336 | bytes 3768320 | tf_op jit(solution)/shard_map/dot_general | solution.py:37
  151.3 0.0 copy-done.4
  151.3 0.0 copy-done.2
  (10 shorter events, 0.1 us)
Async XLA Ops:
  7.2 1.4 copy-start
  7.2 68.3 %reduce-scatter.2.cloned.1.call-start = ((), (), s32[]{:S(2)}) async-start(), calls=%async_computation.6 | async-start | bytes 4718592 | tf_op jit(solution)/shard_map/reduce_scatter | solution.py:31
  12.1 0.8 copy-start.1
  12.2 136.0 %all-gather.2.cloned.1.call-start = ((), (), s32[]{:S(2)}) async-start(), calls=%async_computation.7 | async-start | bytes 2359296 | tf_op jit(solution)/shard_map/all_gather | solution.py:36
  13.1 86.9 %copy-start.5 = (f32[4]{0:T(128)S(1)}, f32[4]{0:T(128)}, u32[]{:S(2)}) copy-start(f32[4]{0:T(128)} %param.8) | copy-start | bytes 52
  34.1 110.7 %copy-start.3 = (f32[4096]{0:T(1024)S(1)}, f32[4096]{0:T(1024)}, u32[]{:S(2)}) copy-start(f32[4096]{0:T(1024)} %param.9) | copy-start | bytes 49156
  100.5 50.7 %copy-start.4 = (f32[4]{0:T(128)}, f32[4]{0:T(128)S(1)}, u32[]{:S(2)}) copy-start(f32[4]{0:T(128)S(1)} %get-tuple-element.16) | copy-start | bytes 52
  145.4 5.8 %copy-start.2 = (f32[4096]{0:T(1024)}, f32[4096]{0:T(1024)S(1)}, u32[]{:S(2)}) copy-start(f32[4096]{0:T(1024)S(1)} %get-tuple-element.14) | copy-start | bytes 49156
Sparse Core Ops, SparseCore 0:
  12.3 63.1 reduce-scatter.1
  77.5 38.9 all-gather.1

commit v2 on v1

--- a/solution.py
+++ b/solution.py
@@ -32,15 +32,14 @@
 
     weight_copy, _ = lax.optimization_barrier((master_weight.astype(jnp.bfloat16), term))
     weight_rows = spread(weight_copy, "z", nz).reshape(nz * rows, cols)
-    weight_rows, part = lax.optimization_barrier((weight_rows, part))
+    terms = lax.all_to_all(part.reshape(nz, rows, cols), "z", 0, 0, tiled=True)
+    weight_rows, terms = lax.optimization_barrier((weight_rows, terms))
     weight = lax.all_gather(weight_rows, "y", axis=0, tiled=True)
     grad_input = lax.dot_general(
         cotangent, weight, (((1,), (1,)), ((), ())), preferred_element_type=jnp.float32
     ).astype(jnp.bfloat16)
 
-    grad = jnp.sum(
-        lax.all_to_all(part.reshape(nz, rows, cols), "z", 0, 0, tiled=True), axis=0
-    )
+    grad = jnp.sum(terms, axis=0)
     squared = grad * grad + EPS1
     row_new = BETA * row_state + (1.0 - BETA) * jnp.sum(squared, axis=1)
     col_part = jnp.sum(squared, axis=0)

time: 160 us -> 161 us (level)
  blocking collectives: 86.8 us -> 41.1 us
  waiting for transfers between devices: 40.6 us -> 67.8 us
  starting transfers between devices: 0.08 us -> 18.2 us
    all_to_all x1 -> x0, blocking collectives: 23 us -> none  [on_device(): lax.all_to_all(part.reshape(nz, rows, cols), 'z', 0, 0, tiled=True)]
    all_to_all x3 -> x2, blocking collectives: 46.8 us -> 25.9 us  [spread(): return lax.all_to_all(copies, axes, 0, 0, tiled=True)]
    all_to_all x0 -> x2, starting transfers between devices: none -> 18.1 us  [the longest x1 11 us: spread(): return lax.all_to_all(copies, axes, 0, 0, tiled=True)]
    all_to_all x0 -> x2, waiting for transfers between devices: none -> 17.1 us  [the longest x1 17.1 us: on_device(): terms = lax.all_to_all(part.reshape(nz, rows, cols), 'z', 0, 0, tiled=True)]
    reduce_scatter x1, waiting for transfers between devices: 40.6 us -> 50.7 us  [on_device(): part = lax.psum_scatter(term, 'y', scatter_dimension=0, tiled=True)]
    all_to_all x1, blocking collectives: 17 us -> 15.2 us  [on_device(): packed = jnp.sum(lax.all_to_all(packed, OTHER, 0, 0, tiled=True), axis=0)]
  transfers between devices with their start and end apart: 2 -> 4, of which waited for: 1 -> 2; matrix products, arithmetic and copies ran while one was open for 4% -> 5% of each run, Pallas kernels for 0% -> 0%
where the time goes in v2:
time: 161 us; the launch traced here: 160 us
  waiting for transfers between devices  67.8 us (42%)
  blocking collectives  41.1 us (26%)
  starting transfers between devices  18.2 us (11%)
  between operations  16.6 us (10%)
  matrix products  6.64 us (4%)
  local copies, waits for them, and re-layouts  6.28 us (4%)
  other arithmetic  3.75 us (2%)
    reduce_scatter x1, waiting for transfers between devices, on_device(): part = lax.psum_scatter(term, 'y', scatter_dimension=0, tiled=True)  50.7 us
    all_to_all x2, blocking collectives, spread(): return lax.all_to_all(copies, axes, 0, 0, tiled=True)  25.9 us
    all_to_all x1, waiting for transfers between devices, on_device(): terms = lax.all_to_all(part.reshape(nz, rows, cols), 'z', 0, 0, tiled=True)  17.1 us
    all_to_all x1, blocking collectives, on_device(): packed = jnp.sum(lax.all_to_all(packed, OTHER, 0, 0, tiled=True), axis=0)  15.2 us
    all_to_all x1, starting transfers between devices, spread(): return lax.all_to_all(copies, axes, 0, 0, tiled=True)  11 us
    all_to_all x1, starting transfers between devices, on_device(): terms = lax.all_to_all(part.reshape(nz, rows, cols), 'z', 0, 0, tiled=True)  7.11 us
    dot_general x1, matrix products, on_device(): lax.dot_general(context, cotangent, (((0,), (0,)), ((), ())), preferred_e...  3.55 us
  transfers between devices with their start and end apart: 4, of which 2 were waited for; matrix products, arithmetic and copies ran while one was open for 5% of the time, Pallas kernels for 0%

profile of v2, /device:TPU:1, one launch (start us, length us, event | category | flops | bytes accessed | tf_op | source)
XLA Modules:
  0.0 160.3 jit_solution(8264046632114908700)
XLA Ops:
  7.2 0.0 copy-start
  7.2 0.0 reduce-scatter.2.cloned.1.call-start
  7.2 1.4 copy-done
  8.6 3.6 %convolution_multiply_fusion = f32[256,4096]{1,0:T(8,128)} fusion(bf16[192,256]{1,0:T(8,128)(2,1)} %param.5, bf16[192,4096]{1,0:T(8,128)(2,1)S(1)} %copy-done), kind=kOutput, calls=%fused_computation | convolution fusion | flops 403701760 | bytes 5865472 | tf_op jit(solution)/shard_map/dot_general | solution.py:26
  12.1 0.0 reduce-scatter.2.cloned.1.call-update
  12.2 0.8 copy-done.1
  13.0 0.8 broadcast_in_dim.6
  13.8 11.0 %all-to-all-start = ((bf16[8,4,4096]{2,1,0:T(4,128)(2,1)}), bf16[8,4,4096]{2,1,0:T(4,128)(2,1)S(1)}, u32[]{:S(2)}, u32[]{:S(2)}) async-start(bf16[8,4,4096]{2,1,0:T(4,128)(2,1)} %broadcast_in_dim.6), calls=%async_computation | async-start | bytes 524288 | tf_op jit(solution)/shard_map/all_to_all | solution.py:14
  24.8 50.7 %reduce-scatter.2.cloned.1.call-done = f32[32,4096]{1,0:T(8,128)} async-done(((f32[256,4096]{1,0:T(8,128)}), f32[32,4096]{1,0:T(8,128)}) %reduce-scatter.2.cloned.1.call-update) | async-done | bytes 524304 | tf_op jit(solution)/shard_map/reduce_scatter | solution.py:31
  75.5 2.0 %reshape.31 = f32[8,4,4096]{2,1,0:T(4,128)} reshape(f32[32,4096]{1,0:T(8,128)} %reduce-scatter.2.cloned.1.call-done) | data formatting | bytes 1048576 | tf_op jit(solution)/shard_map/reshape | solution.py:35
  77.4 0.0 all-to-all-done
  77.4 7.1 %all-to-all-start.1 = ((f32[8,4,4096]{2,1,0:T(4,128)}), f32[8,4,4096]{2,1,0:T(4,128)S(1)}, u32[]{:S(2)}, u32[]{:S(2)}) async-start(f32[8,4,4096]{2,1,0:T(4,128)} %reshape.31), calls=%async_computation.2 | async-start | bytes 1048576 | tf_op jit(solution)/shard_map/all_to_all | solution.py:35
  84.5 0.0 all-gather.2.cloned.1.call-start
  84.6 0.8 reshape.30
  85.4 17.1 %all-to-all-done.1 = f32[8,4,4096]{2,1,0:T(4,128)S(1)} async-done(((f32[8,4,4096]{2,1,0:T(4,128)}), f32[8,4,4096]{2,1,0:T(4,128)S(1)}, u32[]{:S(2)}, u32[]{:S(2)}) %all-to-all-start.1) | async-done | bytes 524320 | tf_op jit(solution)/shard_map/all_to_all | solution.py:35
  102.5 0.0 all-gather.2.cloned.1.call-update
  102.5 0.1 reduce_sum.72
  102.6 0.1 add_reduce_fusion.1
  102.8 0.0 copy-done.5
  102.8 0.6 fusion.1
  103.4 0.1 add_reduce_fusion
  103.5 0.7 select_maximum_fusion
  104.2 15.2 %all_to_all.25 = f32[64,2,128]{2,1,0:T(2,128)S(1)} all-to-all(f32[64,2,128]{2,1,0:T(2,128)S(1)} %select_maximum_fusion), channel_id=1, replica_groups=mesh['y'=8,'z'=8,'x'=4,'c'=2] {'z','x','c'}, dimensions={0} | all-to-all | bytes 131072 | tf_op jit(solution)/shard_map/all_to_all | solution.py:51
  119.4 0.1 reduce_sum.77
  119.5 10.7 %all_to_all.26 = f32[8,2,128]{2,1,0:T(2,128)S(1)} all-to-all(f32[8,2,128]{2,1,0:T(2,128)S(1)} %broadcast_in_dim.7), channel_id=1, replica_groups=mesh['y'=8,'z'=8,'x'=4,'c'=2] {'y'}, dimensions={0} | all-to-all | bytes 16384 | tf_op jit(solution)/shard_map/all_to_all | solution.py:14
  130.2 15.2 %all_to_all.27 = f32[64,2,128]{2,1,0:T(2,128)S(1)} all-to-all(f32[64,2,128]{2,1,0:T(2,128)S(1)} %broadcast_in_dim.8), channel_id=1, replica_groups=mesh['y'=8,'z'=8,'x'=4,'c'=2] {'z','x','c'}, dimensions={0} | all-to-all | bytes 131072 | tf_op jit(solution)/shard_map/all_to_all | solution.py:14
  145.4 0.5 slice.18
  145.9 0.0 copy-done.3
  145.9 0.6 divide_reduce_fusion.1
  147.9 1.4 multiply_divide_fusion
  149.3 3.1 %fusion = bf16[192,256]{1,0:T(8,128)(2,1)} fusion(bf16[256,4096]{1,0:T(8,128)(2,1)} %all-gather.2.cloned.1.call-done, bf16[192,4096]{1,0:T(8,128)(2,1)S(1)} %copy-done), kind=kOutput, calls=%fused_computation.2 | convolution fusion | flops 402702336 | bytes 3768320 | tf_op jit(solution)/shard_map/dot_general | solution.py:38
  152.4 0.0 copy-done.2
  (12 shorter events, 0.1 us)
Async XLA Ops:
  7.2 1.4 copy-start
  7.2 68.3 %reduce-scatter.2.cloned.1.call-start = ((), (), s32[]{:S(2)}) async-start(), calls=%async_computation.6 | async-start | bytes 4718592 | tf_op jit(solution)/shard_map/reduce_scatter | solution.py:31
  12.1 0.8 copy-start.1
  13.8 89.0 %copy-start.5 = (f32[4]{0:T(128)S(1)}, f32[4]{0:T(128)}, u32[]{:S(2)}) copy-start(f32[4]{0:T(128)} %param.8) | copy-start | bytes 52
  13.8 63.7 %all-to-all-start = ((bf16[8,4,4096]{2,1,0:T(4,128)(2,1)}), bf16[8,4,4096]{2,1,0:T(4,128)(2,1)S(1)}, u32[]{:S(2)}, u32[]{:S(2)}) async-start(bf16[8,4,4096]{2,1,0:T(4,128)(2,1)} %broadcast_in_dim.6), calls=%async_computation | async-start | bytes 524288 | tf_op jit(solution)/shard_map/all_to_all | solution.py:14
  24.8 121.2 %copy-start.3 = (f32[4096]{0:T(1024)S(1)}, f32[4096]{0:T(1024)}, u32[]{:S(2)}) copy-start(f32[4096]{0:T(1024)} %param.9) | copy-start | bytes 49156
  77.4 25.1 %all-to-all-start.1 = ((f32[8,4,4096]{2,1,0:T(4,128)}), f32[8,4,4096]{2,1,0:T(4,128)S(1)}, u32[]{:S(2)}, u32[]{:S(2)}) async-start(f32[8,4,4096]{2,1,0:T(4,128)} %reshape.31), calls=%async_computation.2 | async-start | bytes 1048576 | tf_op jit(solution)/shard_map/all_to_all | solution.py:35
  84.5 64.7 %all-gather.2.cloned.1.call-start = ((), (), s32[]{:S(2)}) async-start(), calls=%async_computation.7 | async-start | bytes 2359296 | tf_op jit(solution)/shard_map/all_gather | solution.py:37
  103.4 49.0 %copy-start.4 = (f32[4]{0:T(128)}, f32[4]{0:T(128)S(1)}, u32[]{:S(2)}) copy-start(f32[4]{0:T(128)S(1)} %get-tuple-element.16) | copy-start | bytes 52
  146.5 5.8 %copy-start.2 = (f32[4096]{0:T(1024)}, f32[4096]{0:T(1024)S(1)}, u32[]{:S(2)}) copy-start(f32[4096]{0:T(1024)S(1)} %get-tuple-element.14) | copy-start | bytes 49156
Sparse Core Ops, SparseCore 0:
  12.3 63.1 reduce-scatter.1
  102.7 33.2 all-gather.1

commit v3 on v1

--- a/solution.py
+++ b/solution.py
@@ -22,25 +22,27 @@
     inv_tokens = 1.0 / (cotangent.shape[0] * ny * nz)
     entries = rows * ny * nz * nmp * cols
 
-    term = (
-        lax.dot_general(
-            context, cotangent, (((0,), (0,)), ((), ())), preferred_element_type=jnp.float32
-        )
-        * inv_tokens
-    )
-    part = lax.psum_scatter(term, "y", scatter_dimension=0, tiled=True)
-
-    weight_copy, _ = lax.optimization_barrier((master_weight.astype(jnp.bfloat16), term))
-    weight_rows = spread(weight_copy, "z", nz).reshape(nz * rows, cols)
-    weight_rows, part = lax.optimization_barrier((weight_rows, part))
-    weight = lax.all_gather(weight_rows, "y", axis=0, tiled=True)
+    weight = lax.all_gather(master_weight.astype(jnp.bfloat16), ("y", "z"), axis=0, tiled=True)
     grad_input = lax.dot_general(
         cotangent, weight, (((1,), (1,)), ((), ())), preferred_element_type=jnp.float32
     ).astype(jnp.bfloat16)
 
-    grad = jnp.sum(
-        lax.all_to_all(part.reshape(nz, rows, cols), "z", 0, 0, tiled=True), axis=0
+    bound = (
+        cotangent.shape[0]
+        * jnp.max(jnp.abs(context)).astype(jnp.float32)
+        * jnp.max(jnp.abs(cotangent)).astype(jnp.float32)
     )
+    power = jnp.clip(jnp.floor(jnp.log2(bound)), -100.0, 14.0)
+    term = lax.dot_general(
+        context, cotangent, (((0,), (0,)), ((), ())), preferred_element_type=jnp.float32
+    )
+    coded = (term * jnp.exp2(14.0 - power)).astype(jnp.float16).reshape(ny * nz, rows, cols)
+    coded = jnp.concatenate(
+        [coded, jnp.broadcast_to(power.astype(jnp.float16), (ny * nz, rows, 128))], axis=2
+    )
+    coded = lax.all_to_all(coded, ("y", "z"), 0, 0, tiled=True)
+    scales = jnp.exp2(coded[:, :1, cols:cols + 1].astype(jnp.float32) - 14.0)
+    grad = jnp.sum(coded[:, :, :cols].astype(jnp.float32) * scales, axis=0) * inv_tokens
     squared = grad * grad + EPS1
     row_new = BETA * row_state + (1.0 - BETA) * jnp.sum(squared, axis=1)
     col_part = jnp.sum(squared, axis=0)

time: 160 us -> 190 us (1.19)
  blocking collectives: 86.8 us -> 22.3 us
  waiting for transfers between devices: 40.6 us -> 81.2 us
  starting transfers between devices: 0.08 us -> 36.1 us
  local copies, waits for them, and re-layouts: 4.72 us -> 15 us
  other arithmetic: 3.75 us -> 11 us
    all_to_all x4 -> x0, blocking collectives: 69.8 us -> none  [the longest x3 46.8 us: spread(): return lax.all_to_all(copies, axes, 0, 0, tiled=True)]
    all_to_all x0 -> x3, waiting for transfers between devices: none -> 56.3 us  [the longest x1 49.2 us: on_device(): coded = lax.all_to_all(coded, ('y', 'z'), 0, 0, tiled=True)]
    reduce_scatter x1 -> x0, waiting for transfers between devices: 40.6 us -> none  [on_device(): part = lax.psum_scatter(term, 'y', scatter_dimension=0, tiled=True)]
    all_to_all x0 -> x3, starting transfers between devices: none -> 36 us  [the longest x2 18.5 us: spread(): return lax.all_to_all(copies, axes, 0, 0, tiled=True)]
    all_gather x1, waiting for transfers between devices: 0.01 us -> 24.9 us  [on_device(): lax.all_gather(master_weight.astype(jnp.bfloat16), ('y', 'z'), axis=0, ti...]
    all_to_all x1, blocking collectives: 17 us -> 22.3 us  [on_device(): packed = jnp.sum(lax.all_to_all(packed, OTHER, 0, 0, tiled=True), axis=0)]
    concatenate x0 -> x1, local copies, waits for them, and re-layouts: none -> 4.04 us  [on_device(): jnp.concatenate([coded, jnp.broadcast_to(power.astype(jnp.float16), (ny *...]
    reduce_max x0 -> x2, other arithmetic: none -> 3.85 us  [the longest x1 2.22 us: on_device(): jnp.max(jnp.abs(cotangent)).astype(jnp.float32)]
  transfers between devices with their start and end apart: 2 -> 4, of which waited for: 1 -> 3; matrix products, arithmetic and copies ran while one was open for 4% -> 7% of each run, Pallas kernels for 0% -> 0%
where the time goes in v3:
time: 190 us
  waiting for transfers between devices  81.2 us (43%)
  starting transfers between devices  36.1 us (19%)
  blocking collectives  22.3 us (12%)
  between operations  18 us (9%)
  local copies, waits for them, and re-layouts  15 us (8%)
  other arithmetic  11 us (6%)
  matrix products  6.07 us (3%)
    all_to_all x1, waiting for transfers between devices, on_device(): coded = lax.all_to_all(coded, ('y', 'z'), 0, 0, tiled=True)  49.2 us
    all_gather x1, waiting for transfers between devices, on_device(): lax.all_gather(master_weight.astype(jnp.bfloat16), ('y', 'z'), axis=0, ti...  24.9 us
    all_to_all x1, blocking collectives, on_device(): packed = jnp.sum(lax.all_to_all(packed, OTHER, 0, 0, tiled=True), axis=0)  22.3 us
    all_to_all x2, starting transfers between devices, spread(): return lax.all_to_all(copies, axes, 0, 0, tiled=True)  18.5 us
    all_to_all x1, starting transfers between devices, on_device(): coded = lax.all_to_all(coded, ('y', 'z'), 0, 0, tiled=True)  17.5 us
    all_to_all x2, waiting for transfers between devices, spread(): return lax.all_to_all(copies, axes, 0, 0, tiled=True)  7.01 us
    reshape x1, local copies, waits for them, and re-layouts, on_device(): (term * jnp.exp2(14.0 - power)).astype(jnp.float16)  4.12 us
    unnamed x14, local copies, waits for them, and re-layouts  4.08 us
  transfers between devices with their start and end apart: 4, of which 3 were waited for; matrix products, arithmetic and copies ran while one was open for 7% of the time, Pallas kernels for 0%

profile of v3, /device:TPU:1, one launch (start us, length us, event | category | flops | bytes accessed | tf_op | source)
XLA Modules:
  0.0 189.6 jit_solution(6849981692494900652)
XLA Ops:
  7.2 0.0 copy-start
  7.2 1.6 abs_reduce_fusion.1
  8.8 2.2 %abs_reduce_fusion = bf16[]{:T(256)} fusion(bf16[192,4096]{1,0:T(8,128)(2,1)} %param.6), kind=kLoop, calls=%fused_computation.3 | loop fusion | flops 1572863 | bytes 1572866 | tf_op jit(solution)/shard_map/reduce_max | solution.py:33
  12.4 3.0 %fusion = f16[256,4096]{1,0:T(8,128)(2,1)} fusion(bf16[192,256]{1,0:T(8,128)(2,1)} %param.5, bf16[192,4096]{1,0:T(8,128)(2,1)S(1)} %copy-done, f32[]{:T(128)S(6)} %exp2.16), kind=kOutput, calls=%fused_computation.1 | convolution fusion | flops 404750336 | bytes 3768324 | tf_op jit(solution)/shard_map/dot_general | solution.py:36
  15.4 4.1 %reshape.26 = f16[64,4,4096]{2,1,0:T(4,128)(2,1)} reshape(f16[256,4096]{1,0:T(8,128)(2,1)} %fusion) | data formatting | bytes 4194304 | tf_op jit(solution)/shard_map/reshape | solution.py:39
  19.5 4.0 %concatenate.14 = f16[64,4,4224]{2,1,0:T(4,128)(2,1)} pad(f16[64,4,4096]{2,1,0:T(4,128)(2,1)} %reshape.26, f16[]{:T(256)S(6)} %convert_element_type.29), padding=0_0x0_0x0_128 | pad | bytes 4259842 | tf_op jit(solution)/shard_map/concatenate | solution.py:40
  23.6 17.5 %all-to-all-start = ((f16[64,4,4224]{2,1,0:T(4,128)(2,1)}), f16[64,4,4224]{2,1,0:T(4,128)(2,1)}, u32[]{:S(2)}, u32[]{:S(2)}) async-start(f16[64,4,4224]{2,1,0:T(4,128)(2,1)} %concatenate.14), calls=%async_computation | async-start | bytes 4325376 | tf_op jit(solution)/shard_map/all_to_all | solution.py:43
  41.1 0.0 copy-start.5
  41.1 0.0 all-gather.3.cloned.1.call-start
  41.2 0.6 convert_bitcast_fusion
  41.8 0.0 all-gather.3.cloned.1.call-update
  41.8 49.2 %all-to-all-done = f16[64,4,4224]{2,1,0:T(4,128)(2,1)} async-done(((f16[64,4,4224]{2,1,0:T(4,128)(2,1)}), f16[64,4,4224]{2,1,0:T(4,128)(2,1)}, u32[]{:S(2)}, u32[]{:S(2)}) %all-to-all-start) | async-done | bytes 2162720 | tf_op jit(solution)/shard_map/all_to_all | solution.py:43
  91.1 0.9 slice.26
  92.0 0.1 copy.18
  92.1 2.8 %multiply_reduce_fusion = f32[4,4096]{1,0:T(4,128)S(1)} fusion(f16[64,4,4224]{2,1,0:T(4,128)(2,1)} %all-to-all-done, f32[64]{0:T(128)S(1)} %exponential_bitcast_fusion), kind=kLoop, calls=%fused_computation.2 | loop fusion | flops 3129344 | bytes 2162944 | tf_op jit(solution)/shard_map/reduce_sum | solution.py:45
  94.9 0.1 add_reduce_fusion.1
  95.0 0.6 fusion.1
  95.6 0.1 add_reduce_fusion
  95.8 0.7 select_maximum_fusion
  96.5 22.3 %all_to_all.20 = f32[64,2,128]{2,1,0:T(2,128)S(1)} all-to-all(f32[64,2,128]{2,1,0:T(2,128)S(1)} %select_maximum_fusion), channel_id=1, replica_groups=mesh['y'=8,'z'=8,'x'=4,'c'=2] {'z','x','c'}, dimensions={0} | all-to-all | bytes 131072 | tf_op jit(solution)/shard_map/all_to_all | solution.py:54
  118.8 0.1 reduce_sum.77
  118.9 0.6 broadcast_in_dim.4
  119.5 6.1 %all-to-all-start.2 = ((f32[8,2,128]{2,1,0:T(2,128)}), f32[8,2,128]{2,1,0:T(2,128)S(1)}, u32[]{:S(2)}, u32[]{:S(2)}) async-start(f32[8,2,128]{2,1,0:T(2,128)} %broadcast_in_dim.4), calls=%async_computation.2 | async-start | bytes 16384 | tf_op jit(solution)/shard_map/all_to_all | solution.py:14
  125.5 24.9 %all-gather.3.cloned.1.call-done = bf16[64,4,4096]{2,1,0:T(4,128)(2,1)} async-done(((bf16[1,4,4096]{2,1,0:T(4,128)(2,1)}), bf16[64,4,4096]{2,1,0:T(4,128)(2,1)}) %all-gather.3.cloned.1.call-update) | async-done | bytes 2097168 | tf_op jit(solution)/shard_map/all_gather | solution.py:25
  150.4 4.0 %reshape.28 = bf16[256,4096]{1,0:T(8,128)(2,1)} reshape(bf16[64,4,4096]{2,1,0:T(4,128)(2,1)} %all-gather.3.cloned.1.call-done) | data formatting | bytes 4194304
  154.4 0.7 broadcast_in_dim.5
  155.0 12.5 %all-to-all-start.3 = ((f32[64,2,128]{2,1,0:T(2,128)}), f32[64,2,128]{2,1,0:T(2,128)S(1)}, u32[]{:S(2)}, u32[]{:S(2)}) async-start(f32[64,2,128]{2,1,0:T(2,128)} %broadcast_in_dim.5), calls=%async_computation.3 | async-start | bytes 131072 | tf_op jit(solution)/shard_map/all_to_all | solution.py:14
  167.5 3.1 %convolution_convert_fusion = bf16[192,256]{1,0:T(8,128)(2,1)} fusion(bf16[192,4096]{1,0:T(8,128)(2,1)S(1)} %copy-done, bf16[256,4096]{1,0:T(8,128)(2,1)} %reshape.28), kind=kOutput, calls=%fused_computation.4 | convolution fusion | flops 402702336 | bytes 3768320 | tf_op jit(solution)/shard_map/dot_general | solution.py:26
  170.6 7.0 %all-to-all-done.3 = f32[64,2,128]{2,1,0:T(2,128)S(1)} async-done(((f32[64,2,128]{2,1,0:T(2,128)}), f32[64,2,128]{2,1,0:T(2,128)S(1)}, u32[]{:S(2)}, u32[]{:S(2)}) %all-to-all-start.3) | async-done | bytes 65568 | tf_op jit(solution)/shard_map/all_to_all | solution.py:14
  177.6 0.6 divide_reduce_fusion.1
  178.2 0.6 slice.28
  180.2 1.4 multiply_divide_fusion
  (14 shorter events, 0.1 us)
Async XLA Ops:
  7.2 5.3 %copy-start = (bf16[192,4096]{1,0:T(8,128)(2,1)S(1)}, bf16[192,4096]{1,0:T(8,128)(2,1)}, u32[]{:S(2)}) copy-start(bf16[192,4096]{1,0:T(8,128)(2,1)} %param.6) | copy-start | bytes 4718596
  23.6 17.6 %copy-start.1 = (f32[4,4096]{1,0:T(4,128)S(1)}, f32[4,4096]{1,0:T(4,128)}, u32[]{:S(2)}) copy-start(f32[4,4096]{1,0:T(4,128)} %param.7) | copy-start | bytes 196612
  23.6 67.5 %all-to-all-start = ((f16[64,4,4224]{2,1,0:T(4,128)(2,1)}), f16[64,4,4224]{2,1,0:T(4,128)(2,1)}, u32[]{:S(2)}, u32[]{:S(2)}) async-start(f16[64,4,4224]{2,1,0:T(4,128)(2,1)} %concatenate.14), calls=%async_computation | async-start | bytes 4325376 | tf_op jit(solution)/shard_map/all_to_all | solution.py:43
  41.1 54.0 %copy-start.5 = (f32[4]{0:T(128)S(1)}, f32[4]{0:T(128)}, u32[]{:S(2)}) copy-start(f32[4]{0:T(128)} %param.8) | copy-start | bytes 52
  41.1 109.3 %all-gather.3.cloned.1.call-start = ((), (), s32[]{:S(2)}) async-start(), calls=%async_computation.4 | async-start | bytes 2129920 | tf_op jit(solution)/shard_map/all_gather | solution.py:25
  95.6 84.6 %copy-start.4 = (f32[4]{0:T(128)}, f32[4]{0:T(128)S(1)}, u32[]{:S(2)}) copy-start(f32[4]{0:T(128)S(1)} %get-tuple-element.10) | copy-start | bytes 52
  119.5 34.9 %all-to-all-start.2 = ((f32[8,2,128]{2,1,0:T(2,128)}), f32[8,2,128]{2,1,0:T(2,128)S(1)}, u32[]{:S(2)}, u32[]{:S(2)}) async-start(f32[8,2,128]{2,1,0:T(2,128)} %broadcast_in_dim.4), calls=%async_computation.2 | async-start | bytes 16384 | tf_op jit(solution)/shard_map/all_to_all | solution.py:14
  154.3 23.3 %copy-start.3 = (f32[4096]{0:T(1024)S(1)}, f32[4096]{0:T(1024)}, u32[]{:S(2)}) copy-start(f32[4096]{0:T(1024)} %param.9) | copy-start | bytes 49156
  155.0 22.6 %all-to-all-start.3 = ((f32[64,2,128]{2,1,0:T(2,128)}), f32[64,2,128]{2,1,0:T(2,128)S(1)}, u32[]{:S(2)}, u32[]{:S(2)}) async-start(f32[64,2,128]{2,1,0:T(2,128)} %broadcast_in_dim.5), calls=%async_computation.3 | async-start | bytes 131072 | tf_op jit(solution)/shard_map/all_to_all | solution.py:14
  178.2 3.4 %copy-start.2 = (f32[4096]{0:T(1024)}, f32[4096]{0:T(1024)S(1)}, u32[]{:S(2)}) copy-start(f32[4096]{0:T(1024)S(1)} %get-tuple-element.8) | copy-start | bytes 49156
Sparse Core Ops, SparseCore 0:
  45.5 104.8 all-gather.2

commit v4 on v1

v4 whole, which is shorter than its diff:
```python
import functools

import jax
import jax.numpy as jnp
from jax import lax
from jax.experimental import pallas as pl
from jax.experimental.pallas import tpu as pltpu
from jax.sharding import Mesh, PartitionSpec as P

BETA = 0.8
EPS1 = 1e-30
CLIP = 1.0
CHUNK = 512
LANES = 128
OTHER = ("z", "x", "c")
VMEM = pl.BlockSpec(memory_space=pltpu.VMEM)
PARAMS = pltpu.CompilerParams(vmem_limit_bytes=32 * 2**20)


def term_kernel(inv_tokens, context_ref, left_ref, right_ref, out_ref):
    peers, rows = out_ref.shape[0], out_ref.shape[1] // 2
    for half, cotangent_ref in enumerate((left_ref, right_ref)):
        term = lax.dot_general(
            context_ref[...],
            cotangent_ref[...],
            (((0,), (0,)), ((), ())),
            preferred_element_type=jnp.float32,
        )
        out_ref[:, half * rows:(half + 1) * rows, :] = (term * inv_tokens).reshape(
            peers, rows, term.shape[1]
        )


def term_of(context, cotangent, inv_tokens, peers, rows):
    tokens, cols = cotangent.shape
    steps = cols // (2 * CHUNK)
    return pl.pallas_call(
        functools.partial(term_kernel, inv_tokens),
        grid=(steps,),
        out_shape=jax.ShapeDtypeStruct((peers, 2 * rows, cols // 2), jnp.float32),
        in_specs=[
            pl.BlockSpec((tokens, context.shape[1]), lambda i: (0, 0)),
            pl.BlockSpec((tokens, CHUNK), lambda i: (0, i)),
            pl.BlockSpec((tokens, CHUNK), lambda i: (0, i + steps)),
        ],
        out_specs=pl.BlockSpec((peers, 2 * rows, CHUNK), lambda i: (0, 0, i)),
        compiler_params=pltpu.CompilerParams(vmem_limit_bytes=60 * 2**20),
        cost_estimate=pl.CostEstimate(
            flops=2 * tokens * context.shape[1] * cols,
            bytes_accessed=2 * tokens * cols + 4 * peers * rows * cols,
            transcendentals=0,
        ),
        name="term",
    )(context, cotangent, cotangent)


def sums_kernel(pieces_ref, state_ref, grad_ref, row_ref, packed_ref):
    grad = pieces_ref[0]
    for k in range(1, pieces_ref.shape[0]):
        grad = grad + pieces_ref[k]
    grad_ref[...] = grad
    rows = grad.shape[0] // 2
    plain = grad * grad
    squared = plain + EPS1
    row_sum = jnp.sum(squared, axis=1, keepdims=True)
    row_new = BETA * state_ref[...] + (1.0 - BETA) * (row_sum[:rows] + row_sum[rows:])
    row_ref[...] = row_new
    ratio = plain * (1.0 / jnp.concatenate([row_new, row_new], axis=0))
    per_half = grad.shape[1] // LANES
    packed_ref[:, 1:, :] = jnp.broadcast_to(
        jnp.sum(row_new, axis=0, keepdims=True).reshape(1, 1, 1), (packed_ref.shape[0], 1, LANES)
    )
    for which, value in enumerate((squared, ratio)):
        for half in range(2):
            total = jnp.sum(value[half * rows:(half + 1) * rows], axis=0, keepdims=True)
            for i in range(per_half):
                place = (2 * which + half) * per_half + i
                packed_ref[place, :1, :] = total[:, i * LANES:(i + 1) * LANES]


def sums_of(pieces, row_state, peers):
    count, rows, cols = pieces.shape
    return pl.pallas_call(
        sums_kernel,
        out_shape=(
            jax.ShapeDtypeStruct((rows, cols), jnp.float32),
            jax.ShapeDtypeStruct(row_state.shape, jnp.float32),
            jax.ShapeDtypeStruct((peers, 2, LANES), jnp.float32),
        ),
        in_specs=[VMEM] * 2,
        out_specs=(VMEM,) * 3,
        compiler_params=PARAMS,
        name="sums",
    )(pieces, row_state)


def update_kernel(entries, sums_ref, total_ref, grad_ref, row_ref, state_ref, out_ref, col_ref, rms_ref):
    groups = col_ref.shape[0]
    total = total_ref[:1, :1]
    col_new = BETA * state_ref[...] + (1.0 - BETA) * sums_ref[:groups]
    col_ref[...] = col_new
    ratio = sums_ref[groups:] / col_new
    ratio = jnp.sum(jnp.sum(ratio, axis=0, keepdims=True), axis=1, keepdims=True)
    rms = jnp.sqrt(total * ratio / entries)
    rms_ref[...] = rms
    clip = jnp.maximum(CLIP, rms)
    rows = row_ref.shape[0]
    row = row_ref[...]
    for i in range(groups):
        half, start = divmod(i, groups // 2)
        start *= LANES
        grad = grad_ref[half * rows:(half + 1) * rows, start:start + LANES]
        scaled = grad / jnp.sqrt(row * col_new[i:i + 1] / total)
        out_ref[:, i * LANES:(i + 1) * LANES] = scaled / clip


def update_of(sums, total, grad, row_new, state, entries):
    rows, cols = row_new.shape[0], 2 * grad.shape[1]
    return pl.pallas_call(
        functools.partial(update_kernel, entries),
        out_shape=(
            jax.ShapeDtypeStruct((rows, cols), jnp.float32),
            jax.ShapeDtypeStruct(state.shape, jnp.float32),
            jax.ShapeDtypeStruct((1, 1), jnp.float32),
        ),
        in_specs=[VMEM] * 5,
        out_specs=(VMEM,) * 3,
        compiler_params=PARAMS,
        name="update",
    )(sums, total, grad, row_new, state)


def spread(value, axes, size):
    copies = jnp.broadcast_to(value[None], (size,) + value.shape)
    return lax.all_to_all(copies, axes, 0, 0, tiled=True)


def on_device(context, cotangent, master_weight, row_state, col_state):
    ny, nz = lax.axis_size("y"), lax.axis_size("z")
    nmp = lax.axis_size("x") * lax.axis_size("c")
    n_other = nz * nmp
    rows, cols = master_weight.shape
    inv_tokens = 1.0 / (cotangent.shape[0] * ny * nz)
    entries = rows * ny * nz * nmp * cols

    term = term_of(context, cotangent, inv_tokens, ny * nz, rows)
    part = lax.psum_scatter(
        term.reshape(ny * nz * 2 * rows, cols // 2), "y", scatter_dimension=0, tiled=True
    )

    weight_copy, _ = lax.optimization_barrier((master_weight.astype(jnp.bfloat16), term))
    weight_rows = spread(weight_copy, "z", nz).reshape(nz * rows, cols)
    weight_rows, part = lax.optimization_barrier((weight_rows, part))
    weight = lax.all_gather(weight_rows, "y", axis=0, tiled=True)
    grad_input = lax.dot_general(
        cotangent, weight, (((1,), (1,)), ((), ())), preferred_element_type=jnp.float32
    ).astype(jnp.bfloat16)

    pieces = lax.all_to_all(part.reshape(nz, 2 * rows, cols // 2), "z", 0, 0, tiled=True)
    grad, row_new, packed = sums_of(pieces, row_state[:, None], n_other)
    packed = jnp.sum(lax.all_to_all(packed, OTHER, 0, 0, tiled=True), axis=0)
    packed = jnp.sum(spread(packed, "y", ny), axis=0)
    packed = spread(packed, OTHER, n_other)
    packed, grad_input = lax.optimization_barrier((packed, grad_input))
    update, col_new, update_rms = update_of(
        packed[:, 0], packed[0, 1:], grad, row_new, col_state.reshape(cols // LANES, LANES), entries
    )
    return (grad_input, update, row_new[:, 0], col_new.reshape(cols), update_rms[0, 0])


def solution(mesh):
    grid = Mesh(mesh.devices.reshape(8, 8, 4, 2), ("y", "z", "x", "c"))
    dp, mp = ("y", "z"), ("x", "c")
    in_specs = (P(dp, mp), P(dp, None), P(mp + dp, None), P(mp + dp), P())
    out_specs = (P(dp, mp), P(mp + dp, None), P(mp + dp), P(), P())
    return jax.shard_map(
        on_device, mesh=grid, in_specs=in_specs, out_specs=out_specs, check_vma=False
    )
```

time: 160 us -> 153 us (0.956)
  blocking collectives: 86.8 us -> 36.2 us
  waiting for transfers between devices: 40.6 us -> 71.4 us
  starting transfers between devices: 0.08 us -> 17.4 us
  Pallas kernels: 0 us -> 6.02 us
  matrix products: 6.64 us -> 3.08 us
  other arithmetic: 3.75 us -> 0.74 us
  between operations: 16.6 us -> 14.1 us
  local copies, waits for them, and re-layouts: 4.72 us -> 2.98 us
    all_to_all x0 -> x3, waiting for transfers between devices: none -> 30.8 us  [the longest x1 17.9 us: on_device(): lax.all_to_all(part.reshape(nz, 2 * rows, cols // 2), 'z', 0, 0, tiled=True)]
    all_to_all x3 -> x1, blocking collectives: 46.8 us -> 21 us  [spread(): return lax.all_to_all(copies, axes, 0, 0, tiled=True)]
    all_to_all x1 -> x0, blocking collectives: 23 us -> none  [on_device(): lax.all_to_all(part.reshape(nz, rows, cols), 'z', 0, 0, tiled=True)]
    all_to_all x0 -> x3, starting transfers between devices: none -> 17.3 us  [the longest x2 10.2 us: spread(): return lax.all_to_all(copies, axes, 0, 0, tiled=True)]
    pallas_call x0 -> x3, Pallas kernels: none -> 6.02 us  [the longest x1 4.96 us: term_of(): pl.pallas_call(functools.partial(term_kernel, inv_tokens), grid=(steps,),...]
    dot_general x1 -> x0, matrix products: 3.55 us -> none  [on_device(): lax.dot_general(context, cotangent, (((0,), (0,)), ((), ())), preferred_e...]
    all_to_all x1, blocking collectives: 17 us -> 15.2 us  [on_device(): packed = jnp.sum(lax.all_to_all(packed, OTHER, 0, 0, tiled=True), axis=0)]
  transfers between devices with their start and end apart: 2 -> 5, of which waited for: 1 -> 4; matrix products, arithmetic and copies ran while one was open for 4% -> 4% of each run, Pallas kernels for 0% -> 0%
where the time goes in v4:
time: 153 us; the launch traced here: 152 us
  waiting for transfers between devices  71.4 us (47%)
  blocking collectives  36.2 us (24%)
  starting transfers between devices  17.4 us (11%)
  between operations  14.1 us (9%)
  Pallas kernels  6.02 us (4%)
  matrix products  3.08 us (2%)
  local copies, waits for them, and re-layouts  2.98 us (2%)
    reduce_scatter x1, waiting for transfers between devices, on_device(): lax.psum_scatter(term.reshape(ny * nz * 2 * rows, cols // 2), 'y', scatte...  40.6 us
    all_to_all x1, blocking collectives, spread(): return lax.all_to_all(copies, axes, 0, 0, tiled=True)  21 us
    all_to_all x1, waiting for transfers between devices, on_device(): lax.all_to_all(part.reshape(nz, 2 * rows, cols // 2), 'z', 0, 0, tiled=True)  17.9 us
    all_to_all x1, blocking collectives, on_device(): packed = jnp.sum(lax.all_to_all(packed, OTHER, 0, 0, tiled=True), axis=0)  15.2 us
    all_to_all x2, waiting for transfers between devices, spread(): return lax.all_to_all(copies, axes, 0, 0, tiled=True)  13 us
    all_to_all x2, starting transfers between devices, spread(): return lax.all_to_all(copies, axes, 0, 0, tiled=True)  10.2 us
    all_to_all x1, starting transfers between devices, on_device(): lax.all_to_all(part.reshape(nz, 2 * rows, cols // 2), 'z', 0, 0, tiled=True)  7.12 us
    pallas_call x1, Pallas kernels, term_of(): pl.pallas_call(functools.partial(term_kernel, inv_tokens), grid=(steps,),...  4.96 us
  transfers between devices with their start and end apart: 5, of which 4 were waited for; matrix products, arithmetic and copies ran while one was open for 4% of the time, Pallas kernels for 0%

profile of v4, /device:TPU:1, one launch (start us, length us, event | category | flops | bytes accessed | tf_op | source)
XLA Modules:
  0.0 152.0 jit_solution(6101293355535362219)
XLA Ops:
  7.2 0.0 reduce-scatter.2.cloned.1.call-start
  7.2 5.0 %term.1 = f32[64,8,2048]{2,1,0:T(8,128)} custom-call(bf16[192,256]{1,0:T(8,128)(2,1)} %context_ref.1, bf16[192,4096]{1,0:T(8,128)(2,1)} %right_ref.1, bf16[192,4096]{1,0:T(8,128)(2,1)} %right_ref.1), custom_call_target="tpu_custom_call" | custom-call | flops 402653184 | bytes 5767168 | tf_op jit(solution)/shard_map/term/pallas_call | solution.py:37
  12.2 0.0 copy-start.2
  12.2 0.0 reduce-scatter.2.cloned.1.call-update
  12.2 0.0 copy-start.3
  12.2 0.0 copy-start.1
  12.2 0.0 all-gather.2.cloned.1.call-start
  12.3 0.7 copy-done.2
  13.0 0.1 broadcast_in_dim.8
  13.1 21.0 %all_to_all.25 = bf16[8,4,4096]{2,1,0:T(4,128)(2,1)S(1)} all-to-all(bf16[8,4,4096]{2,1,0:T(4,128)(2,1)S(1)} %broadcast_in_dim.8), channel_id=1, replica_groups=mesh['y'=8,'z'=8,'x'=4,'c'=2] {'z'}, dimensions={0} | all-to-all | bytes 524288 | tf_op jit(solution)/shard_map/all_to_all | solution.py:135
  34.2 0.8 reshape.28
  34.9 40.6 %reduce-scatter.2.cloned.1.call-done = f32[64,2048]{1,0:T(8,128)} async-done(((f32[512,2048]{1,0:T(8,128)}), f32[64,2048]{1,0:T(8,128)}) %reduce-scatter.2.cloned.1.call-update) | async-done | bytes 524304 | tf_op jit(solution)/shard_map/reduce_scatter | solution.py:147
  75.5 0.0 all-gather.2.cloned.1.call-update
  75.5 7.1 %all-to-all-start.1 = ((f32[8,8,2048]{2,1,0:T(8,128)}), f32[8,8,2048]{2,1,0:T(8,128)S(1)}, u32[]{:S(2)}, u32[]{:S(2)}) async-start(f32[8,8,2048]{2,1,0:T(8,128)} %bitcast.16), calls=%async_computation.2 | async-start | bytes 1048576 | tf_op jit(solution)/shard_map/all_to_all | solution.py:159
  82.6 0.0 copy-done.3
  82.6 0.1 copy.16.state_ref
  82.7 17.9 %all-to-all-done.1.pieces_ref = f32[8,8,2048]{2,1,0:T(8,128)S(1)} async-done(((f32[8,8,2048]{2,1,0:T(8,128)}), f32[8,8,2048]{2,1,0:T(8,128)S(1)}, u32[]{:S(2)}, u32[]{:S(2)}) %all-to-all-start.1) | async-done | bytes 524320 | tf_op jit(solution)/shard_map/all_to_all | solution.py:159
  100.6 0.2 sums.1
  100.8 15.2 %all_to_all.26 = f32[64,2,128]{2,1,0:T(2,128)S(1)} all-to-all(f32[64,2,128]{2,1,0:T(2,128)S(1)} %get-tuple-element.18), channel_id=1, replica_groups=mesh['y'=8,'z'=8,'x'=4,'c'=2] {'z','x','c'}, dimensions={0} | all-to-all | bytes 131072 | tf_op jit(solution)/shard_map/all_to_all | solution.py:161
  116.0 0.1 reduce_sum.18
  116.1 0.6 broadcast_in_dim.10
  116.7 4.3 %all-to-all-start.3 = ((f32[8,2,128]{2,1,0:T(2,128)}), f32[8,2,128]{2,1,0:T(2,128)S(1)}, u32[]{:S(2)}, u32[]{:S(2)}) async-start(f32[8,2,128]{2,1,0:T(2,128)} %broadcast_in_dim.10), calls=%async_computation.4 | async-start | bytes 16384 | tf_op jit(solution)/shard_map/all_to_all | solution.py:135
  121.1 0.6 reduce
  121.7 5.9 %all-to-all-done.3 = f32[8,2,128]{2,1,0:T(2,128)S(1)} async-done(((f32[8,2,128]{2,1,0:T(2,128)}), f32[8,2,128]{2,1,0:T(2,128)S(1)}, u32[]{:S(2)}, u32[]{:S(2)}) %all-to-all-start.3) | async-done | bytes 8224 | tf_op jit(solution)/shard_map/all_to_all | solution.py:135
  127.7 0.7 broadcast_in_dim.11
  128.3 5.9 %all-to-all-start.4 = ((f32[64,2,128]{2,1,0:T(2,128)}), f32[64,2,128]{2,1,0:T(2,128)S(1)}, u32[]{:S(2)}, u32[]{:S(2)}) async-start(f32[64,2,128]{2,1,0:T(2,128)} %broadcast_in_dim.11), calls=%async_computation.5 | async-start | bytes 131072 | tf_op jit(solution)/shard_map/all_to_all | solution.py:135
  134.2 0.0 all-gather.2.cloned.1.call-done
  134.2 0.0 copy-done.1
  134.2 3.1 %fusion = bf16[192,256]{1,0:T(8,128)(2,1)} fusion(bf16[256,4096]{1,0:T(8,128)(2,1)} %all-gather.2.cloned.1.call-done, bf16[192,4096]{1,0:T(8,128)(2,1)S(1)} %copy-done.1), kind=kOutput, calls=%fused_computation.1 | convolution fusion | flops 402702336 | bytes 3768320 | tf_op jit(solution)/shard_map/dot_general | solution.py:155
  137.3 7.0 %all-to-all-done.4 = f32[64,2,128]{2,1,0:T(2,128)S(1)} async-done(((f32[64,2,128]{2,1,0:T(2,128)}), f32[64,2,128]{2,1,0:T(2,128)S(1)}, u32[]{:S(2)}, u32[]{:S(2)}) %all-to-all-start.4) | async-done | bytes 65568 | tf_op jit(solution)/shard_map/all_to_all | solution.py:135
  144.3 0.0 copy-done
  144.4 0.8 update.1
  (6 shorter events, 0.0 us)
Async XLA Ops:
  7.2 68.3 %reduce-scatter.2.cloned.1.call-start = ((), (), s32[]{:S(2)}) async-start(), calls=%async_computation.6 | async-start | bytes 4718592 | tf_op jit(solution)/shard_map/reduce_scatter | solution.py:147
  12.2 0.8 copy-start.2
  12.2 70.4 %copy-start.3 = (f32[4]{0:T(128)S(1)}, f32[4]{0:T(128)}, u32[]{:S(2)}) copy-start(f32[4]{0:T(128)} %param.8) | copy-start | bytes 52
  12.2 122.0 %copy-start.1 = (bf16[192,4096]{1,0:T(8,128)(2,1)S(1)}, bf16[192,4096]{1,0:T(8,128)(2,1)}, u32[]{:S(2)}) copy-start(bf16[192,4096]{1,0:T(8,128)(2,1)} %right_ref.1) | copy-start | bytes 4718596
  12.2 122.0 %all-gather.2.cloned.1.call-start = ((), (), s32[]{:S(2)}) async-start(), calls=%async_computation.7 | async-start | bytes 2359296 | tf_op jit(solution)/shard_map/all_gather | solution.py:154
  75.5 25.1 %all-to-all-start.1 = ((f32[8,8,2048]{2,1,0:T(8,128)}), f32[8,8,2048]{2,1,0:T(8,128)S(1)}, u32[]{:S(2)}, u32[]{:S(2)}) async-start(f32[8,8,2048]{2,1,0:T(8,128)} %bitcast.16), calls=%async_computation.2 | async-start | bytes 1048576 | tf_op jit(solution)/shard_map/all_to_all | solution.py:159
  116.7 27.6 %copy-start = (f32[4096]{0:T(1024)S(1)}, f32[4096]{0:T(1024)}, u32[]{:S(2)}) copy-start(f32[4096]{0:T(1024)} %param.9) | copy-start | bytes 49156
  116.7 10.9 %all-to-all-start.3 = ((f32[8,2,128]{2,1,0:T(2,128)}), f32[8,2,128]{2,1,0:T(2,128)S(1)}, u32[]{:S(2)}, u32[]{:S(2)}) async-start(f32[8,2,128]{2,1,0:T(2,128)} %broadcast_in_dim.10), calls=%async_computation.4 | async-start | bytes 16384 | tf_op jit(solution)/shard_map/all_to_all | solution.py:135
  128.3 16.0 %all-to-all-start.4 = ((f32[64,2,128]{2,1,0:T(2,128)}), f32[64,2,128]{2,1,0:T(2,128)S(1)}, u32[]{:S(2)}, u32[]{:S(2)}) async-start(f32[64,2,128]{2,1,0:T(2,128)} %broadcast_in_dim.11), calls=%async_computation.5 | async-start | bytes 131072 | tf_op jit(solution)/shard_map/all_to_all | solution.py:135
Sparse Core Ops, SparseCore 0:
  12.3 63.1 reduce-scatter.1
  77.6 39.0 all-gather.1

commit v5 on v4

--- a/solution.py
+++ b/solution.py
@@ -12,7 +12,8 @@
 CLIP = 1.0
 CHUNK = 512
 LANES = 128
-OTHER = ("z", "x", "c")
+NEAR = ("x", "c")
+FAR = ("y", "z")
 VMEM = pl.BlockSpec(memory_space=pltpu.VMEM)
 PARAMS = pltpu.CompilerParams(vmem_limit_bytes=32 * 2**20)
 
@@ -67,15 +68,13 @@
     row_ref[...] = row_new
     ratio = plain * (1.0 / jnp.concatenate([row_new, row_new], axis=0))
     per_half = grad.shape[1] // LANES
-    packed_ref[:, 1:, :] = jnp.broadcast_to(
-        jnp.sum(row_new, axis=0, keepdims=True).reshape(1, 1, 1), (packed_ref.shape[0], 1, LANES)
-    )
     for which, value in enumerate((squared, ratio)):
         for half in range(2):
             total = jnp.sum(value[half * rows:(half + 1) * rows], axis=0, keepdims=True)
             for i in range(per_half):
                 place = (2 * which + half) * per_half + i
-                packed_ref[place, :1, :] = total[:, i * LANES:(i + 1) * LANES]
+                group, line = divmod(place, packed_ref.shape[1])
+                packed_ref[group, line:line + 1, :] = total[:, i * LANES:(i + 1) * LANES]
 
 
 def sums_of(pieces, row_state, peers):
@@ -85,7 +84,7 @@
         out_shape=(
             jax.ShapeDtypeStruct((rows, cols), jnp.float32),
             jax.ShapeDtypeStruct(row_state.shape, jnp.float32),
-            jax.ShapeDtypeStruct((peers, 2, LANES), jnp.float32),
+            jax.ShapeDtypeStruct((peers, 2 * 2 * cols // (peers * LANES), LANES), jnp.float32),
         ),
         in_specs=[VMEM] * 2,
         out_specs=(VMEM,) * 3,
@@ -96,7 +95,8 @@
 
 def update_kernel(entries, sums_ref, total_ref, grad_ref, row_ref, state_ref, out_ref, col_ref, rms_ref):
     groups = col_ref.shape[0]
-    total = total_ref[:1, :1]
+    total = jnp.sum(jnp.sum(sums_ref[:groups], axis=0, keepdims=True), axis=1, keepdims=True)
+    total = BETA * total_ref[:1, :1] + (1.0 - BETA) * total
     col_new = BETA * state_ref[...] + (1.0 - BETA) * sums_ref[:groups]
     col_ref[...] = col_new
     ratio = sums_ref[groups:] / col_new
@@ -130,15 +130,29 @@
     )(sums, total, grad, row_new, state)
 
 
-def spread(value, axes, size):
-    copies = jnp.broadcast_to(value[None], (size,) + value.shape)
-    return lax.all_to_all(copies, axes, 0, 0, tiled=True)
+def fold_kernel(value_ref, out_ref):
+    total = jnp.sum(value_ref[...], axis=0, keepdims=True)
+    out_ref[...] = jnp.broadcast_to(total, out_ref.shape)
+
+
+def fold(value, copies):
+    return pl.pallas_call(
+        fold_kernel,
+        out_shape=jax.ShapeDtypeStruct((copies,) + value.shape[1:], value.dtype),
+        in_specs=[VMEM],
+        out_specs=VMEM,
+        compiler_params=PARAMS,
+        name="fold",
+    )(value)
+
+
+def exchange(value, axes):
+    return lax.all_to_all(value, axes, 0, 0, tiled=True)
 
 
 def on_device(context, cotangent, master_weight, row_state, col_state):
     ny, nz = lax.axis_size("y"), lax.axis_size("z")
     nmp = lax.axis_size("x") * lax.axis_size("c")
-    n_other = nz * nmp
     rows, cols = master_weight.shape
     inv_tokens = 1.0 / (cotangent.shape[0] * ny * nz)
     entries = rows * ny * nz * nmp * cols
@@ -148,22 +162,27 @@
         term.reshape(ny * nz * 2 * rows, cols // 2), "y", scatter_dimension=0, tiled=True
     )
 
-    weight_copy, _ = lax.optimization_barrier((master_weight.astype(jnp.bfloat16), term))
-    weight_rows = spread(weight_copy, "z", nz).reshape(nz * rows, cols)
-    weight_rows, part = lax.optimization_barrier((weight_rows, part))
+    weight_copy, row_state, _ = lax.optimization_barrier(
+        (master_weight.astype(jnp.bfloat16), row_state, term)
+    )
+    copies = jnp.broadcast_to(weight_copy[None], (nz, rows, cols))
+    weight_rows = exchange(copies, "z").reshape(nz * rows, cols)
+    state_sum = jnp.broadcast_to(jnp.sum(row_state), (nmp, 1, LANES))
+    state_sum = fold(exchange(fold(exchange(state_sum, NEAR), ny * nz), FAR), 1)[0]
+    weight_rows, part, state_sum = lax.optimization_barrier((weight_rows, part, state_sum))
     weight = lax.all_gather(weight_rows, "y", axis=0, tiled=True)
     grad_input = lax.dot_general(
         cotangent, weight, (((1,), (1,)), ((), ())), preferred_element_type=jnp.float32
     ).astype(jnp.bfloat16)
 
-    pieces = lax.all_to_all(part.reshape(nz, 2 * rows, cols // 2), "z", 0, 0, tiled=True)
-    grad, row_new, packed = sums_of(pieces, row_state[:, None], n_other)
-    packed = jnp.sum(lax.all_to_all(packed, OTHER, 0, 0, tiled=True), axis=0)
-    packed = jnp.sum(spread(packed, "y", ny), axis=0)
-    packed = spread(packed, OTHER, n_other)
+    pieces = exchange(part.reshape(nz, 2 * rows, cols // 2), "z")
+    grad, row_new, packed = sums_of(pieces, row_state[:, None], nmp)
+    packed = fold(exchange(packed, NEAR), ny * nz)
+    packed = fold(exchange(packed, FAR), nmp)
+    packed = exchange(packed, NEAR).reshape(2 * cols // LANES, LANES)
     packed, grad_input = lax.optimization_barrier((packed, grad_input))
     update, col_new, update_rms = update_of(
-        packed[:, 0], packed[0, 1:], grad, row_new, col_state.reshape(cols // LANES, LANES), entries
+        packed, state_sum, grad, row_new, col_state.reshape(cols // LANES, LANES), entries
     )
     return (grad_input, update, row_new[:, 0], col_new.reshape(cols), update_rms[0, 0])
 

time: 153 us -> 150 us (0.980)
  waiting for transfers between devices: 71.4 us -> 51.4 us
  blocking collectives: 36.2 us -> 46.8 us
  starting transfers between devices: 17.4 us -> 22.1 us
  Pallas kernels: 6.02 us -> 7.59 us
    reduce_scatter x1, waiting for transfers between devices: 40.6 us -> 10.1 us  [on_device(): lax.psum_scatter(term.reshape(ny * nz * 2 * rows, cols // 2), 'y', scatte...]
    all_to_all x2 -> x3, blocking collectives: 36.2 us -> 46.8 us  [exchange(): return lax.all_to_all(value, axes, 0, 0, tiled=True)]
    all_to_all x3 -> x4, waiting for transfers between devices: 30.8 us -> 41.3 us  [exchange(): return lax.all_to_all(value, axes, 0, 0, tiled=True)]
    all_to_all x3 -> x4, starting transfers between devices: 17.3 us -> 22.1 us  [exchange(): return lax.all_to_all(value, axes, 0, 0, tiled=True)]
  transfers between devices with their start and end apart: 5 -> 6, of which waited for: 4 -> 5; matrix products, arithmetic and copies ran while one was open for 4% -> 4% of each run, Pallas kernels for 0% -> 1%
where the time goes in v5:
time: 150 us
  waiting for transfers between devices  51.4 us (34%)
  blocking collectives  46.8 us (31%)
  starting transfers between devices  22.1 us (15%)
  between operations  14.1 us (9%)
  Pallas kernels  7.59 us (5%)
  local copies, waits for them, and re-layouts  3.11 us (2%)
  matrix products  3.08 us (2%)
    all_to_all x3, blocking collectives, exchange(): return lax.all_to_all(value, axes, 0, 0, tiled=True)  46.8 us
    all_to_all x4, waiting for transfers between devices, exchange(): return lax.all_to_all(value, axes, 0, 0, tiled=True)  41.3 us
    all_to_all x4, starting transfers between devices, exchange(): return lax.all_to_all(value, axes, 0, 0, tiled=True)  22.1 us
    reduce_scatter x1, waiting for transfers between devices, on_device(): lax.psum_scatter(term.reshape(ny * nz * 2 * rows, cols // 2), 'y', scatte...  10.1 us
    pallas_call x1, Pallas kernels, term_of(): pl.pallas_call(functools.partial(term_kernel, inv_tokens), grid=(steps,),...  5 us
    dot_general x1, matrix products, on_device(): lax.dot_general(cotangent, weight, (((1,), (1,)), ((), ())), preferred_el...  3.08 us
  transfers between devices with their start and end apart: 6, of which 5 were waited for; matrix products, arithmetic and copies ran while one was open for 4% of the time, Pallas kernels for 1%

profile of v5, /device:TPU:1, one launch (start us, length us, event | category | flops | bytes accessed | tf_op | source)
XLA Modules:
  0.0 149.5 jit_solution(2570096081837138739)
XLA Ops:
  7.2 0.0 reduce-scatter.2.cloned.1.call-start
  7.2 5.0 %term.1 = f32[64,8,2048]{2,1,0:T(8,128)} custom-call(bf16[192,256]{1,0:T(8,128)(2,1)} %context_ref.1, bf16[192,4096]{1,0:T(8,128)(2,1)} %right_ref.1, bf16[192,4096]{1,0:T(8,128)(2,1)} %right_ref.1), custom_call_target="tpu_custom_call" | custom-call | flops 402653184 | bytes 5767168 | tf_op jit(solution)/shard_map/term/pallas_call | solution.py:38
  12.2 0.0 reduce-scatter.2.cloned.1.call-update
  12.2 0.8 copy-done.2
  13.1 0.0 copy-done.3
  13.1 0.6 reduce_sum.9
  13.7 0.6 broadcast_in_dim.13
  14.3 13.8 %all_to_all.35.value_ref = f32[8,1,128]{2,1,0:T(1,128)S(1)} all-to-all(f32[8,1,128]{2,1,0:T(1,128)S(1)} %broadcast_in_dim.13), channel_id=1, replica_groups=mesh['y'=8,'z'=8,'x'=4,'c'=2] {'x','c'}, dimensions={0} | all-to-all | bytes 8192 | tf_op jit(solution)/shard_map/all_to_all | solution.py:150
  28.2 23.8 %all_to_all.36.value_ref = f32[64,1,128]{2,1,0:T(1,128)S(1)} all-to-all(f32[64,1,128]{2,1,0:T(1,128)S(1)} %fold.4), channel_id=1, replica_groups=mesh['y'=8,'z'=8,'x'=4,'c'=2] {'y','z'}, dimensions={0} | all-to-all | bytes 65536 | tf_op jit(solution)/shard_map/all_to_all | solution.py:150
  51.9 0.8 broadcast_in_dim.12
  52.7 3.5 %all-to-all-start = ((bf16[8,4,4096]{2,1,0:T(4,128)(2,1)}), bf16[8,4,4096]{2,1,0:T(4,128)(2,1)S(1)}, u32[]{:S(2)}, u32[]{:S(2)}) async-start(bf16[8,4,4096]{2,1,0:T(4,128)(2,1)} %broadcast_in_dim.12), calls=%async_computation | async-start | bytes 524288 | tf_op jit(solution)/shard_map/all_to_all | solution.py:150
  56.3 0.0 all-gather.2.cloned.1.call-start
  56.3 0.1 fold.5
  56.4 9.1 %all-to-all-done = bf16[8,4,4096]{2,1,0:T(4,128)(2,1)S(1)} async-done(((bf16[8,4,4096]{2,1,0:T(4,128)(2,1)}), bf16[8,4,4096]{2,1,0:T(4,128)(2,1)S(1)}, u32[]{:S(2)}, u32[]{:S(2)}) %all-to-all-start) | async-done | bytes 262176 | tf_op jit(solution)/shard_map/all_to_all | solution.py:150
  65.5 0.8 reshape.29
  66.2 10.1 %reduce-scatter.2.cloned.1.call-done = f32[64,2048]{1,0:T(8,128)} async-done(((f32[512,2048]{1,0:T(8,128)}), f32[64,2048]{1,0:T(8,128)}) %reduce-scatter.2.cloned.1.call-update) | async-done | bytes 524304 | tf_op jit(solution)/shard_map/reduce_scatter | solution.py:161
  76.3 0.0 all-gather.2.cloned.1.call-update
  76.3 7.1 %all-to-all-start.3 = ((f32[8,8,2048]{2,1,0:T(8,128)}), f32[8,8,2048]{2,1,0:T(8,128)S(1)}, u32[]{:S(2)}, u32[]{:S(2)}) async-start(f32[8,8,2048]{2,1,0:T(8,128)} %bitcast.16), calls=%async_computation.4 | async-start | bytes 1048576 | tf_op jit(solution)/shard_map/all_to_all | solution.py:150
  83.4 0.1 copy.11.state_ref
  83.5 17.9 %all-to-all-done.3.pieces_ref = f32[8,8,2048]{2,1,0:T(8,128)S(1)} async-done(((f32[8,8,2048]{2,1,0:T(8,128)}), f32[8,8,2048]{2,1,0:T(8,128)S(1)}, u32[]{:S(2)}, u32[]{:S(2)}) %all-to-all-start.3) | async-done | bytes 524320 | tf_op jit(solution)/shard_map/all_to_all | solution.py:150
  101.4 0.2 sums.1
  101.6 9.3 %all_to_all.37.value_ref = f32[8,8,128]{2,1,0:T(8,128)S(1)} all-to-all(f32[8,8,128]{2,1,0:T(8,128)S(1)} %get-tuple-element.21), channel_id=1, replica_groups=mesh['y'=8,'z'=8,'x'=4,'c'=2] {'x','c'}, dimensions={0} | all-to-all | bytes 65536 | tf_op jit(solution)/shard_map/all_to_all | solution.py:150
  110.9 0.7 fold.6
  111.6 5.3 %all-to-all-start.5 = ((f32[64,8,128]{2,1,0:T(8,128)}), f32[64,8,128]{2,1,0:T(8,128)S(1)}, u32[]{:S(2)}, u32[]{:S(2)}) async-start(f32[64,8,128]{2,1,0:T(8,128)} %fold.6), calls=%async_computation.6 | async-start | bytes 524288 | tf_op jit(solution)/shard_map/all_to_all | solution.py:150
  116.9 0.0 copy-start
  116.9 0.6 reduce
  117.6 12.7 %all-to-all-done.5.value_ref = f32[64,8,128]{2,1,0:T(8,128)S(1)} async-done(((f32[64,8,128]{2,1,0:T(8,128)}), f32[64,8,128]{2,1,0:T(8,128)S(1)}, u32[]{:S(2)}, u32[]{:S(2)}) %all-to-all-start.5) | async-done | bytes 262176 | tf_op jit(solution)/shard_map/all_to_all | solution.py:150
  130.2 0.7 fold.7
  130.9 6.2 %all-to-all-start.6 = ((f32[8,8,128]{2,1,0:T(8,128)}), f32[8,8,128]{2,1,0:T(8,128)S(1)}, u32[]{:S(2)}, u32[]{:S(2)}) async-start(f32[8,8,128]{2,1,0:T(8,128)} %fold.7), calls=%async_computation.7 | async-start | bytes 65536 | tf_op jit(solution)/shard_map/all_to_all | solution.py:150
  137.1 3.1 %fusion = bf16[192,256]{1,0:T(8,128)(2,1)} fusion(bf16[256,4096]{1,0:T(8,128)(2,1)} %all-gather.2.cloned.1.call-done, bf16[192,4096]{1,0:T(8,128)(2,1)S(1)} %copy-done.1), kind=kOutput, calls=%fused_computation.1 | convolution fusion | flops 402702336 | bytes 3768320 | tf_op jit(solution)/shard_map/dot_general | solution.py:174
  140.2 1.6 %all-to-all-done.6 = f32[8,8,128]{2,1,0:T(8,128)S(1)} async-done(((f32[8,8,128]{2,1,0:T(8,128)}), f32[8,8,128]{2,1,0:T(8,128)S(1)}, u32[]{:S(2)}, u32[]{:S(2)}) %all-to-all-start.6) | async-done | bytes 32800 | tf_op jit(solution)/shard_map/all_to_all | solution.py:150
  141.8 0.9 update.1
  (8 shorter events, 0.1 us)
Async XLA Ops:
  7.2 69.2 %reduce-scatter.2.cloned.1.call-start = ((), (), s32[]{:S(2)}) async-start(), calls=%async_computation.8 | async-start | bytes 4718592 | tf_op jit(solution)/shard_map/reduce_scatter | solution.py:161
  12.2 0.8 copy-start.2
  12.2 0.9 copy-start.3
  52.7 84.4 %copy-start.1 = (bf16[192,4096]{1,0:T(8,128)(2,1)S(1)}, bf16[192,4096]{1,0:T(8,128)(2,1)}, u32[]{:S(2)}) copy-start(bf16[192,4096]{1,0:T(8,128)(2,1)} %right_ref.1) | copy-start | bytes 4718596
  52.7 12.8 %all-to-all-start = ((bf16[8,4,4096]{2,1,0:T(4,128)(2,1)}), bf16[8,4,4096]{2,1,0:T(4,128)(2,1)S(1)}, u32[]{:S(2)}, u32[]{:S(2)}) async-start(bf16[8,4,4096]{2,1,0:T(4,128)(2,1)} %broadcast_in_dim.12), calls=%async_computation | async-start | bytes 524288 | tf_op jit(solution)/shard_map/all_to_all | solution.py:150
  56.3 80.8 %all-gather.2.cloned.1.call-start = ((), (), s32[]{:S(2)}) async-start(), calls=%async_computation.9 | async-start | bytes 2359296 | tf_op jit(solution)/shard_map/all_gather | solution.py:173
  76.3 25.1 %all-to-all-start.3 = ((f32[8,8,2048]{2,1,0:T(8,128)}), f32[8,8,2048]{2,1,0:T(8,128)S(1)}, u32[]{:S(2)}, u32[]{:S(2)}) async-start(f32[8,8,2048]{2,1,0:T(8,128)} %bitcast.16), calls=%async_computation.4 | async-start | bytes 1048576 | tf_op jit(solution)/shard_map/all_to_all | solution.py:150
  111.6 18.6 %all-to-all-start.5 = ((f32[64,8,128]{2,1,0:T(8,128)}), f32[64,8,128]{2,1,0:T(8,128)S(1)}, u32[]{:S(2)}, u32[]{:S(2)}) async-start(f32[64,8,128]{2,1,0:T(8,128)} %fold.6), calls=%async_computation.6 | async-start | bytes 524288 | tf_op jit(solution)/shard_map/all_to_all | solution.py:150
  116.9 24.9 %copy-start = (f32[4096]{0:T(1024)S(1)}, f32[4096]{0:T(1024)}, u32[]{:S(2)}) copy-start(f32[4096]{0:T(1024)} %param.9) | copy-start | bytes 49156
  130.9 10.9 %all-to-all-start.6 = ((f32[8,8,128]{2,1,0:T(8,128)}), f32[8,8,128]{2,1,0:T(8,128)S(1)}, u32[]{:S(2)}, u32[]{:S(2)}) async-start(f32[8,8,128]{2,1,0:T(8,128)} %fold.7), calls=%async_computation.7 | async-start | bytes 65536 | tf_op jit(solution)/shard_map/all_to_all | solution.py:150
Sparse Core Ops, SparseCore 0:
  12.4 63.9 reduce-scatter.1
  78.4 39.0 all-gather.1

commit v6 on v5

--- a/solution.py
+++ b/solution.py
@@ -11,6 +11,7 @@
 EPS1 = 1e-30
 CLIP = 1.0
 CHUNK = 512
+ASIDE = 384
 LANES = 128
 NEAR = ("x", "c")
 FAR = ("y", "z")
@@ -18,33 +19,70 @@
 PARAMS = pltpu.CompilerParams(vmem_limit_bytes=32 * 2**20)
 
 
-def term_kernel(inv_tokens, context_ref, left_ref, right_ref, out_ref):
-    peers, rows = out_ref.shape[0], out_ref.shape[1] // 2
-    for half, cotangent_ref in enumerate((left_ref, right_ref)):
-        term = lax.dot_general(
-            context_ref[...],
-            cotangent_ref[...],
-            (((0,), (0,)), ((), ())),
-            preferred_element_type=jnp.float32,
+def spans(start, stop):
+    return [(i, min(CHUNK, stop - i)) for i in range(start, stop, CHUNK)]
+
+
+def product(context_ref, cotangent, inv_tokens):
+    return inv_tokens * lax.dot_general(
+        context_ref[...], cotangent, (((0,), (0,)), ((), ())), preferred_element_type=jnp.float32
+    )
+
+
+def term_kernel(inv_tokens, context_hbm, cotangent_hbm, state_ref, out_hbm, context_ref, cotangent_ref, out_ref, in_sems, out_sems):
+    peers, rows, width = out_ref.shape[0], out_ref.shape[1] // 2, out_ref.shape[2] - LANES
+    half_cols = cotangent_hbm.shape[1] // 2
+    first = pltpu.make_async_copy(context_hbm, context_ref, in_sems.at[0])
+    first.start()
+    loads = []
+    for k, (start, size) in enumerate(spans(0, width)):
+        for half in range(2):
+            place = pl.ds(half * half_cols + start, size)
+            copy = pltpu.make_async_copy(
+                cotangent_hbm.at[:, place], cotangent_ref.at[:, place], in_sems.at[1 + 2 * k + half]
+            )
+            copy.start()
+            loads.append(copy)
+    first.wait()
+    stores = []
+    for k, (start, size) in enumerate(spans(0, width)):
+        for half in range(2):
+            loads[2 * k + half].wait()
+            place = half * half_cols + start
+            term = product(context_ref, cotangent_ref[:, place:place + size], inv_tokens)
+            out_ref[:, half * rows:(half + 1) * rows, start:start + size] = term.reshape(
+                peers, rows, size
+            )
+        if start + size == width:
+            total = jnp.sum(state_ref[...], axis=1, keepdims=True).reshape(1, 1, 1)
+            out_ref[:, :, width:] = jnp.broadcast_to(total, (peers, 2 * rows, LANES))
+            size += LANES
+        place = pl.ds(start, size)
+        copy = pltpu.make_async_copy(
+            out_ref.at[:, :, place], out_hbm.at[:, :, place], out_sems.at[k]
         )
-        out_ref[:, half * rows:(half + 1) * rows, :] = (term * inv_tokens).reshape(
-            peers, rows, term.shape[1]
-        )
-
-
-def term_of(context, cotangent, inv_tokens, peers, rows):
+        copy.start()
+        stores.append(copy)
+    for copy in stores:
+        copy.wait()
+
+
+def term_of(context, cotangent, row_state, inv_tokens, peers, rows):
     tokens, cols = cotangent.shape
-    steps = cols // (2 * CHUNK)
+    width = cols // 2 - ASIDE + LANES
+    count = len(spans(0, width - LANES))
     return pl.pallas_call(
         functools.partial(term_kernel, inv_tokens),
-        grid=(steps,),
-        out_shape=jax.ShapeDtypeStruct((peers, 2 * rows, cols // 2), jnp.float32),
-        in_specs=[
-            pl.BlockSpec((tokens, context.shape[1]), lambda i: (0, 0)),
-            pl.BlockSpec((tokens, CHUNK), lambda i: (0, i)),
-            pl.BlockSpec((tokens, CHUNK), lambda i: (0, i + steps)),
+        out_shape=jax.ShapeDtypeStruct((peers, 2 * rows, width), jnp.float32),
+        in_specs=[pl.BlockSpec(memory_space=pl.ANY)] * 2 + [VMEM],
+        out_specs=pl.BlockSpec(memory_space=pl.ANY),
+        scratch_shapes=[
+            pltpu.VMEM(context.shape, context.dtype),
+            pltpu.VMEM(cotangent.shape, cotangent.dtype),
+            pltpu.VMEM((peers, 2 * rows, width), jnp.float32),
+            pltpu.SemaphoreType.DMA((1 + 2 * count,)),
+            pltpu.SemaphoreType.DMA((count,)),
         ],
-        out_specs=pl.BlockSpec((peers, 2 * rows, CHUNK), lambda i: (0, 0, i)),
         compiler_params=pltpu.CompilerParams(vmem_limit_bytes=60 * 2**20),
         cost_estimate=pl.CostEstimate(
             flops=2 * tokens * context.shape[1] * cols,
@@ -52,14 +90,40 @@
             transcendentals=0,
         ),
         name="term",
-    )(context, cotangent, cotangent)
-
-
-def sums_kernel(pieces_ref, state_ref, grad_ref, row_ref, packed_ref):
-    grad = pieces_ref[0]
-    for k in range(1, pieces_ref.shape[0]):
-        grad = grad + pieces_ref[k]
+    )(context, cotangent, row_state[None])
+
+
+def aside_kernel(inv_tokens, context_ref, left_ref, right_ref, out_ref):
+    nz, ny, rows, width = out_ref.shape
+    rows //= 2
+    for half, cotangent_ref in enumerate((left_ref, right_ref)):
+        term = product(context_ref, cotangent_ref[...], inv_tokens)
+        for y in range(ny):
+            part = term[y * nz * rows:(y + 1) * nz * rows]
+            out_ref[:, y, half * rows:(half + 1) * rows, :] = part.reshape(nz, rows, width)
+
+
+def aside_of(context, cotangent, inv_tokens, ny, nz, rows):
+    half_cols = cotangent.shape[1] // 2
+    left = cotangent[:, half_cols - ASIDE:half_cols]
+    right = cotangent[:, 2 * half_cols - ASIDE:]
+    return pl.pallas_call(
+        functools.partial(aside_kernel, inv_tokens),
+        out_shape=jax.ShapeDtypeStruct((nz, ny, 2 * rows, ASIDE), jnp.float32),
+        in_specs=[VMEM] * 3,
+        out_specs=VMEM,
+        compiler_params=PARAMS,
+        name="aside",
+    )(context, left, right)
+
+
+def sums_kernel(pieces_ref, aside_ref, state_ref, grad_ref, row_ref, packed_ref):
+    most = jnp.sum(pieces_ref[...], axis=0)
+    width = most.shape[1] - LANES
+    grad = jnp.concatenate([most[:, :width], jnp.sum(aside_ref[...], axis=0)], axis=1)
     grad_ref[...] = grad
+    lines = packed_ref.shape[1] // 2
+    packed_ref[:, lines:, :] = jnp.broadcast_to(most[None, :lines, width:], (packed_ref.shape[0], lines, LANES))
     rows = grad.shape[0] // 2
     plain = grad * grad
     squared = plain + EPS1
@@ -73,24 +137,24 @@
             total = jnp.sum(value[half * rows:(half + 1) * rows], axis=0, keepdims=True)
             for i in range(per_half):
                 place = (2 * which + half) * per_half + i
-                group, line = divmod(place, packed_ref.shape[1])
+                group, line = divmod(place, lines)
                 packed_ref[group, line:line + 1, :] = total[:, i * LANES:(i + 1) * LANES]
 
 
-def sums_of(pieces, row_state, peers):
-    count, rows, cols = pieces.shape
+def sums_of(pieces, aside, row_state, peers):
+    rows, cols = pieces.shape[1], pieces.shape[2] - LANES + ASIDE
     return pl.pallas_call(
         sums_kernel,
         out_shape=(
             jax.ShapeDtypeStruct((rows, cols), jnp.float32),
             jax.ShapeDtypeStruct(row_state.shape, jnp.float32),
-            jax.ShapeDtypeStruct((peers, 2 * 2 * cols // (peers * LANES), LANES), jnp.float32),
-        ),
-        in_specs=[VMEM] * 2,
+            jax.ShapeDtypeStruct((peers, 2 * 4 * cols // (peers * LANES), LANES), jnp.float32),
+        ),
+        in_specs=[VMEM] * 3,
         out_specs=(VMEM,) * 3,
         compiler_params=PARAMS,
         name="sums",
-    )(pieces, row_state)
+    )(pieces, aside, row_state)
 
 
 def update_kernel(entries, sums_ref, total_ref, grad_ref, row_ref, state_ref, out_ref, col_ref, rms_ref):
@@ -146,6 +210,28 @@
     )(value)
 
 
+def split_kernel(value_ref, out_ref, rest_ref):
+    total = jnp.sum(value_ref[...], axis=0, keepdims=True)
+    lines = out_ref.shape[1]
+    out_ref[...] = jnp.broadcast_to(total[:, :lines], out_ref.shape)
+    rest_ref[...] = total[0, lines:]
+
+
+def split_fold(value, copies):
+    lines = value.shape[1] // 2
+    return pl.pallas_call(
+        split_kernel,
+        out_shape=(
+            jax.ShapeDtypeStruct((copies, lines, LANES), value.dtype),
+            jax.ShapeDtypeStruct((lines, LANES), value.dtype),
+        ),
+        in_specs=[VMEM],
+        out_specs=(VMEM,) * 2,
+        compiler_params=PARAMS,
+        name="split_fold",
+    )(value)
+
+
 def exchange(value, axes):
     return lax.all_to_all(value, axes, 0, 0, tiled=True)
 
@@ -157,27 +243,26 @@
     inv_tokens = 1.0 / (cotangent.shape[0] * ny * nz)
     entries = rows * ny * nz * nmp * cols
 
-    term = term_of(context, cotangent, inv_tokens, ny * nz, rows)
+    term = term_of(context, cotangent, row_state, inv_tokens, ny * nz, rows)
     part = lax.psum_scatter(
-        term.reshape(ny * nz * 2 * rows, cols // 2), "y", scatter_dimension=0, tiled=True
-    )
-
-    weight_copy, row_state, _ = lax.optimization_barrier(
-        (master_weight.astype(jnp.bfloat16), row_state, term)
+        term.reshape(ny * nz * 2 * rows, term.shape[2]), "y", scatter_dimension=0, tiled=True
+    )
+    weight_copy, context, _ = lax.optimization_barrier(
+        (master_weight.astype(jnp.bfloat16), context, term)
     )
     copies = jnp.broadcast_to(weight_copy[None], (nz, rows, cols))
     weight_rows = exchange(copies, "z").reshape(nz * rows, cols)
-    state_sum = jnp.broadcast_to(jnp.sum(row_state), (nmp, 1, LANES))
-    state_sum = fold(exchange(fold(exchange(state_sum, NEAR), ny * nz), FAR), 1)[0]
-    weight_rows, part, state_sum = lax.optimization_barrier((weight_rows, part, state_sum))
+    aside = exchange(aside_of(context, cotangent, inv_tokens, ny, nz, rows), "z")
+    aside = exchange(jnp.sum(aside, axis=0), "y")
+    weight_rows, part, aside = lax.optimization_barrier((weight_rows, part, aside))
     weight = lax.all_gather(weight_rows, "y", axis=0, tiled=True)
     grad_input = lax.dot_general(
         cotangent, weight, (((1,), (1,)), ((), ())), preferred_element_type=jnp.float32
     ).astype(jnp.bfloat16)
 
-    pieces = exchange(part.reshape(nz, 2 * rows, cols // 2), "z")
-    grad, row_new, packed = sums_of(pieces, row_state[:, None], nmp)
-    packed = fold(exchange(packed, NEAR), ny * nz)
+    pieces = exchange(part.reshape(nz, 2 * rows, term.shape[2]), "z")
+    grad, row_new, packed = sums_of(pieces, aside, row_state[:, None], nmp)
+    packed, state_sum = split_fold(exchange(packed, NEAR), ny * nz)
     packed = fold(exchange(packed, FAR), nmp)
     packed = exchange(packed, NEAR).reshape(2 * cols // LANES, LANES)
     packed, grad_input = lax.optimization_barrier((packed, grad_input))

time: 150 us -> 145 us (0.967)
  waiting for transfers between devices: 51.4 us -> 42.7 us
  starting transfers between devices: 22.1 us -> 27 us
    reduce_scatter x1, waiting for transfers between devices: 10.1 us -> 0.01 us  [on_device(): lax.psum_scatter(term.reshape(ny * nz * 2 * rows, term.shape[2]), 'y', sc...]
    all_to_all x4 -> x5, starting transfers between devices: 22.1 us -> 26.9 us  [exchange(): return lax.all_to_all(value, axes, 0, 0, tiled=True)]
    all_to_all x4 -> x5, waiting for transfers between devices: 41.3 us -> 42.6 us  [exchange(): return lax.all_to_all(value, axes, 0, 0, tiled=True)]
    all_to_all x3 -> x2, blocking collectives: 46.8 us -> 45.8 us  [exchange(): return lax.all_to_all(value, axes, 0, 0, tiled=True)]
    pallas_call x1 -> x3, Pallas kernels: 5 us -> 5.77 us  [the longest x1 4.7 us: term_of(): pl.pallas_call(functools.partial(term_kernel, inv_tokens), out_shape=jax....]
  transfers between devices with their start and end apart: 6 -> 7, of which waited for: 5 -> 5; matrix products, arithmetic and copies ran while one was open for 4% -> 4% of each run, Pallas kernels for 1% -> 1%
where the time goes in v6:
time: 145 us
  blocking collectives  45.8 us (32%)
  waiting for transfers between devices  42.7 us (29%)
  starting transfers between devices  27 us (19%)
  between operations  14.1 us (10%)
  Pallas kernels  7.5 us (5%)
  matrix products  3.08 us (2%)
  local copies, waits for them, and re-layouts  3.05 us (2%)
    all_to_all x2, blocking collectives, exchange(): return lax.all_to_all(value, axes, 0, 0, tiled=True)  45.8 us
    all_to_all x5, waiting for transfers between devices, exchange(): return lax.all_to_all(value, axes, 0, 0, tiled=True)  42.6 us
    all_to_all x5, starting transfers between devices, exchange(): return lax.all_to_all(value, axes, 0, 0, tiled=True)  26.9 us
    pallas_call x1, Pallas kernels, term_of(): pl.pallas_call(functools.partial(term_kernel, inv_tokens), out_shape=jax....  4.7 us
    dot_general x1, matrix products, on_device(): lax.dot_general(cotangent, weight, (((1,), (1,)), ((), ())), preferred_el...  3.08 us
  transfers between devices with their start and end apart: 7, of which 5 were waited for; matrix products, arithmetic and copies ran while one was open for 4% of the time, Pallas kernels for 1%

profile of v6, /device:TPU:1, one launch (start us, length us, event | category | flops | bytes accessed | tf_op | source)
XLA Modules:
  0.0 144.6 jit_solution(5275141500057524689)
XLA Ops:
  7.2 0.0 reduce-scatter.2.cloned.1.call-start
  7.2 4.7 %term.1 = f32[64,8,1792]{2,1,0:T(8,128)} custom-call(bf16[192,256]{1,0:T(8,128)(2,1)} %context_ref, bf16[192,4096]{1,0:T(8,128)(2,1)} %cotangent_hbm.1, f32[1,4]{1,0:T(1,128)} %bitcast.16), custom_call_target="tpu_custom_call" | custom-call | flops 402653184 | bytes 5767168 | tf_op jit(solution)/shard_map/term/pallas_call | solution.py:74
  11.9 0.0 copy-start.2
  11.9 0.0 copy-start
  12.0 0.0 reduce-scatter.2.cloned.1.call-update
  12.0 0.8 copy-done.3
  12.8 0.6 copy-done.2
  13.4 0.3 aside.1
  13.7 32.3 %all_to_all.35 = f32[8,8,8,384]{3,2,1,0:T(8,128)S(1)} all-to-all(f32[8,8,8,384]{3,2,1,0:T(8,128)S(1)} %aside.1), channel_id=1, replica_groups=mesh['y'=8,'z'=8,'x'=4,'c'=2] {'z'}, dimensions={0} | all-to-all | bytes 1572864 | tf_op jit(solution)/shard_map/all_to_all | solution.py:236
  46.0 0.8 broadcast_in_dim.13
  46.8 3.4 %all-to-all-start = ((bf16[8,4,4096]{2,1,0:T(4,128)(2,1)}), bf16[8,4,4096]{2,1,0:T(4,128)(2,1)S(1)}, u32[]{:S(2)}, u32[]{:S(2)}) async-start(bf16[8,4,4096]{2,1,0:T(4,128)(2,1)} %broadcast_in_dim.13), calls=%async_computation | async-start | bytes 524288 | tf_op jit(solution)/shard_map/all_to_all | solution.py:236
  50.2 0.7 reduce_sum.9
  50.9 8.7 %all-to-all-done = bf16[8,4,4096]{2,1,0:T(4,128)(2,1)S(1)} async-done(((bf16[8,4,4096]{2,1,0:T(4,128)(2,1)}), bf16[8,4,4096]{2,1,0:T(4,128)(2,1)S(1)}, u32[]{:S(2)}, u32[]{:S(2)}) %all-to-all-start) | async-done | bytes 262176 | tf_op jit(solution)/shard_map/all_to_all | solution.py:236
  59.5 6.8 %all-to-all-start.2 = ((f32[8,8,384]{2,1,0:T(8,128)}), f32[8,8,384]{2,1,0:T(8,128)S(1)}, u32[]{:S(2)}, u32[]{:S(2)}) async-start(f32[8,8,384]{2,1,0:T(8,128)} %reduce_sum.9), calls=%async_computation.3 | async-start | bytes 196608 | tf_op jit(solution)/shard_map/all_to_all | solution.py:236
  66.4 0.0 all-gather.2.cloned.1.call-start
  66.4 0.8 reshape.29
  67.2 6.8 %all-to-all-done.2.aside_ref = f32[8,8,384]{2,1,0:T(8,128)S(1)} async-done(((f32[8,8,384]{2,1,0:T(8,128)}), f32[8,8,384]{2,1,0:T(8,128)S(1)}, u32[]{:S(2)}, u32[]{:S(2)}) %all-to-all-start.2) | async-done | bytes 98336 | tf_op jit(solution)/shard_map/all_to_all | solution.py:236
  74.0 0.0 all-gather.2.cloned.1.call-update
  74.0 5.2 %all-to-all-start.3 = ((f32[8,8,1792]{2,1,0:T(8,128)}), f32[8,8,1792]{2,1,0:T(8,128)S(1)}, u32[]{:S(2)}, u32[]{:S(2)}) async-start(f32[8,8,1792]{2,1,0:T(8,128)} %bitcast.15), calls=%async_computation.4 | async-start | bytes 917504 | tf_op jit(solution)/shard_map/all_to_all | solution.py:236
  79.1 0.1 copy.11.state_ref
  79.2 12.3 %all-to-all-done.3.pieces_ref = f32[8,8,1792]{2,1,0:T(8,128)S(1)} async-done(((f32[8,8,1792]{2,1,0:T(8,128)}), f32[8,8,1792]{2,1,0:T(8,128)S(1)}, u32[]{:S(2)}, u32[]{:S(2)}) %all-to-all-start.3) | async-done | bytes 458784 | tf_op jit(solution)/shard_map/all_to_all | solution.py:236
  91.5 0.2 sums.1
  91.7 13.6 %all_to_all.36.value_ref = f32[8,16,128]{2,1,0:T(8,128)S(1)} all-to-all(f32[8,16,128]{2,1,0:T(8,128)S(1)} %get-tuple-element.24), channel_id=1, replica_groups=mesh['y'=8,'z'=8,'x'=4,'c'=2] {'x','c'}, dimensions={0} | all-to-all | bytes 131072 | tf_op jit(solution)/shard_map/all_to_all | solution.py:236
  105.3 0.7 split_fold.1
  106.1 5.8 %all-to-all-start.5 = ((f32[64,8,128]{2,1,0:T(8,128)}), f32[64,8,128]{2,1,0:T(8,128)S(1)}, u32[]{:S(2)}, u32[]{:S(2)}) async-start(f32[64,8,128]{2,1,0:T(8,128)} %get-tuple-element.25), calls=%async_computation.6 | async-start | bytes 524288 | tf_op jit(solution)/shard_map/all_to_all | solution.py:236
  111.8 0.6 reduce
  112.5 13.3 %all-to-all-done.5.value_ref = f32[64,8,128]{2,1,0:T(8,128)S(1)} async-done(((f32[64,8,128]{2,1,0:T(8,128)}), f32[64,8,128]{2,1,0:T(8,128)S(1)}, u32[]{:S(2)}, u32[]{:S(2)}) %all-to-all-start.5) | async-done | bytes 262176 | tf_op jit(solution)/shard_map/all_to_all | solution.py:236
  125.7 0.7 fold.1
  126.4 5.8 %all-to-all-start.6 = ((f32[8,8,128]{2,1,0:T(8,128)}), f32[8,8,128]{2,1,0:T(8,128)S(1)}, u32[]{:S(2)}, u32[]{:S(2)}) async-start(f32[8,8,128]{2,1,0:T(8,128)} %fold.1), calls=%async_computation.7 | async-start | bytes 65536 | tf_op jit(solution)/shard_map/all_to_all | solution.py:236
  132.2 3.1 %fusion = bf16[192,256]{1,0:T(8,128)(2,1)} fusion(bf16[256,4096]{1,0:T(8,128)(2,1)} %all-gather.2.cloned.1.call-done, bf16[192,4096]{1,0:T(8,128)(2,1)S(1)} %copy-done.2), kind=kOutput, calls=%fused_computation.1 | convolution fusion | flops 402702336 | bytes 3768320 | tf_op jit(solution)/shard_map/dot_general | solution.py:259
  135.3 1.7 %all-to-all-done.6 = f32[8,8,128]{2,1,0:T(8,128)S(1)} async-done(((f32[8,8,128]{2,1,0:T(8,128)}), f32[8,8,128]{2,1,0:T(8,128)S(1)}, u32[]{:S(2)}, u32[]{:S(2)}) %all-to-all-start.6) | async-done | bytes 32800 | tf_op jit(solution)/shard_map/all_to_all | solution.py:236
  136.9 0.8 update.1
  (10 shorter events, 0.1 us)
Async XLA Ops:
  7.2 66.8 %reduce-scatter.2.cloned.1.call-start = ((), (), s32[]{:S(2)}) async-start(), calls=%async_computation.8 | async-start | bytes 4128768 | tf_op jit(solution)/shard_map/reduce_scatter | solution.py:247
  11.9 0.8 copy-start.3
  11.9 1.4 copy-start.2
  11.9 1.5 %copy-start = (bf16[192,256]{1,0:T(8,128)(2,1)S(1)}, bf16[192,256]{1,0:T(8,128)(2,1)}, u32[]{:S(2)}) copy-start(bf16[192,256]{1,0:T(8,128)(2,1)} %context_ref) | copy-start | bytes 294916
  46.0 33.1 %copy-start.4 = (f32[4]{0:T(128)S(1)}, f32[4]{0:T(128)}, u32[]{:S(2)}) copy-start(f32[4]{0:T(128)} %param.8) | copy-start | bytes 52
  46.8 12.8 %all-to-all-start = ((bf16[8,4,4096]{2,1,0:T(4,128)(2,1)}), bf16[8,4,4096]{2,1,0:T(4,128)(2,1)S(1)}, u32[]{:S(2)}, u32[]{:S(2)}) async-start(bf16[8,4,4096]{2,1,0:T(4,128)(2,1)} %broadcast_in_dim.13), calls=%async_computation | async-start | bytes 524288 | tf_op jit(solution)/shard_map/all_to_all | solution.py:236
  59.5 14.4 %all-to-all-start.2 = ((f32[8,8,384]{2,1,0:T(8,128)}), f32[8,8,384]{2,1,0:T(8,128)S(1)}, u32[]{:S(2)}, u32[]{:S(2)}) async-start(f32[8,8,384]{2,1,0:T(8,128)} %reduce_sum.9), calls=%async_computation.3 | async-start | bytes 196608 | tf_op jit(solution)/shard_map/all_to_all | solution.py:236
  66.4 65.8 %all-gather.2.cloned.1.call-start = ((), (), s32[]{:S(2)}) async-start(), calls=%async_computation.9 | async-start | bytes 2359296 | tf_op jit(solution)/shard_map/all_gather | solution.py:258
  74.0 17.5 %all-to-all-start.3 = ((f32[8,8,1792]{2,1,0:T(8,128)}), f32[8,8,1792]{2,1,0:T(8,128)S(1)}, u32[]{:S(2)}, u32[]{:S(2)}) async-start(f32[8,8,1792]{2,1,0:T(8,128)} %bitcast.15), calls=%async_computation.4 | async-start | bytes 917504 | tf_op jit(solution)/shard_map/all_to_all | solution.py:236
  106.1 19.7 %all-to-all-start.5 = ((f32[64,8,128]{2,1,0:T(8,128)}), f32[64,8,128]{2,1,0:T(8,128)S(1)}, u32[]{:S(2)}, u32[]{:S(2)}) async-start(f32[64,8,128]{2,1,0:T(8,128)} %get-tuple-element.25), calls=%async_computation.6 | async-start | bytes 524288 | tf_op jit(solution)/shard_map/all_to_all | solution.py:236
  111.8 25.1 %copy-start.1 = (f32[4096]{0:T(1024)S(1)}, f32[4096]{0:T(1024)}, u32[]{:S(2)}) copy-start(f32[4096]{0:T(1024)} %param.9) | copy-start | bytes 49156
  126.4 10.5 %all-to-all-start.6 = ((f32[8,8,128]{2,1,0:T(8,128)}), f32[8,8,128]{2,1,0:T(8,128)S(1)}, u32[]{:S(2)}, u32[]{:S(2)}) async-start(f32[8,8,128]{2,1,0:T(8,128)} %fold.1), calls=%async_computation.7 | async-start | bytes 65536 | tf_op jit(solution)/shard_map/all_to_all | solution.py:236
Sparse Core Ops, SparseCore 0:
  12.1 58.1 reduce-scatter.1
  74.1 39.8 all-gather.1

commit v7 on v6

--- a/solution.py
+++ b/solution.py
@@ -11,7 +11,7 @@
 EPS1 = 1e-30
 CLIP = 1.0
 CHUNK = 512
-ASIDE = 384
+ASIDE = 512
 LANES = 128
 NEAR = ("x", "c")
 FAR = ("y", "z")
@@ -93,28 +93,75 @@
     )(context, cotangent, row_state[None])
 
 
-def aside_kernel(inv_tokens, context_ref, left_ref, right_ref, out_ref):
-    nz, ny, rows, width = out_ref.shape
+def aside_kernel(inv_tokens, context_ref, left_ref, right_ref, weight_ref, out_ref, term_ref):
+    nz, ny, rows, _ = term_ref.shape
     rows //= 2
     for half, cotangent_ref in enumerate((left_ref, right_ref)):
         term = product(context_ref, cotangent_ref[...], inv_tokens)
         for y in range(ny):
             part = term[y * nz * rows:(y + 1) * nz * rows]
-            out_ref[:, y, half * rows:(half + 1) * rows, :] = part.reshape(nz, rows, width)
-
-
-def aside_of(context, cotangent, inv_tokens, ny, nz, rows):
-    half_cols = cotangent.shape[1] // 2
-    left = cotangent[:, half_cols - ASIDE:half_cols]
-    right = cotangent[:, 2 * half_cols - ASIDE:]
+            term_ref[:, y, half * rows:(half + 1) * rows, :] = part.reshape(nz, rows, ASIDE)
+    for z in range(nz):
+        term = term_ref[z]
+        upper = term.astype(jnp.bfloat16).astype(jnp.float32)
+        both = jnp.concatenate([upper, term - upper], axis=1)
+        out_ref[z, :, :, :ASIDE] = both.astype(jnp.bfloat16)
+    size = out_ref.shape[3] - ASIDE
+    groups = out_ref.shape[2] // rows
+    for y in range(ny):
+        starts = [(y * groups + q) * size for q in range(groups)]
+        part = jnp.concatenate([weight_ref[:, i:i + size] for i in starts], axis=0)
+        out_ref[:, y, :, ASIDE:] = jnp.broadcast_to(part[None], (nz,) + part.shape).astype(
+            jnp.bfloat16
+        )
+
+
+def aside_of(context, cotangent, weight, inv_tokens, ny, nz):
+    rows, cols = weight.shape
+    left = cotangent[:, cols // 2 - ASIDE:cols // 2]
+    right = cotangent[:, cols - ASIDE:]
     return pl.pallas_call(
         functools.partial(aside_kernel, inv_tokens),
-        out_shape=jax.ShapeDtypeStruct((nz, ny, 2 * rows, ASIDE), jnp.float32),
-        in_specs=[VMEM] * 3,
+        out_shape=jax.ShapeDtypeStruct(
+            (nz, ny, 4 * rows, ASIDE + cols // (4 * ny)), jnp.bfloat16
+        ),
+        in_specs=[VMEM] * 4,
         out_specs=VMEM,
+        scratch_shapes=[pltpu.VMEM((nz, ny, 2 * rows, ASIDE), jnp.float32)],
         compiler_params=PARAMS,
         name="aside",
-    )(context, left, right)
+    )(context, left, right, weight)
+
+
+def arrival_kernel(value_ref, sum_ref, weight_ref):
+    nz, ny, lines, width = value_ref.shape
+    rows = lines // 4
+    size = width - ASIDE
+    total = value_ref[0, :, :, :ASIDE].astype(jnp.float32)
+    for z in range(1, nz):
+        total = total + value_ref[z, :, :, :ASIDE].astype(jnp.float32)
+    sum_ref[...] = total[:, :2 * rows] + total[:, 2 * rows:]
+    for y in range(ny):
+        part = value_ref[:, y, :, ASIDE:].astype(jnp.float32)
+        for q in range(4):
+            start = (y * 4 + q) * size
+            block = part[:, q * rows:(q + 1) * rows].reshape(nz * rows, size)
+            weight_ref[:, start:start + size] = block.astype(jnp.bfloat16)
+
+
+def arrival(value):
+    nz, ny, lines, width = value.shape
+    return pl.pallas_call(
+        arrival_kernel,
+        out_shape=(
+            jax.ShapeDtypeStruct((ny, lines // 2, ASIDE), jnp.float32),
+            jax.ShapeDtypeStruct((nz * lines // 4, 4 * ny * (width - ASIDE)), jnp.bfloat16),
+        ),
+        in_specs=[VMEM],
+        out_specs=(VMEM,) * 2,
+        compiler_params=PARAMS,
+        name="arrival",
+    )(value)
 
 
 def sums_kernel(pieces_ref, aside_ref, state_ref, grad_ref, row_ref, packed_ref):
@@ -247,13 +294,10 @@
     part = lax.psum_scatter(
         term.reshape(ny * nz * 2 * rows, term.shape[2]), "y", scatter_dimension=0, tiled=True
     )
-    weight_copy, context, _ = lax.optimization_barrier(
-        (master_weight.astype(jnp.bfloat16), context, term)
-    )
-    copies = jnp.broadcast_to(weight_copy[None], (nz, rows, cols))
-    weight_rows = exchange(copies, "z").reshape(nz * rows, cols)
-    aside = exchange(aside_of(context, cotangent, inv_tokens, ny, nz, rows), "z")
-    aside = exchange(jnp.sum(aside, axis=0), "y")
+    context, _ = lax.optimization_barrier((context, term))
+    aside = aside_of(context, cotangent, master_weight, inv_tokens, ny, nz)
+    aside, weight_rows = arrival(exchange(aside, "z"))
+    aside = exchange(aside, "y")
     weight_rows, part, aside = lax.optimization_barrier((weight_rows, part, aside))
     weight = lax.all_gather(weight_rows, "y", axis=0, tiled=True)
     grad_input = lax.dot_general(

time: 145 us -> 143 us (0.986)
  blocking collectives: 45.8 us -> 70.1 us
  waiting for transfers between devices: 42.7 us -> 27.8 us
  starting transfers between devices: 27 us -> 16.9 us
  local copies, waits for them, and re-layouts: 3.05 us -> 1.44 us
    all_to_all x2 -> x3, blocking collectives: 45.8 us -> 70.1 us  [exchange(): return lax.all_to_all(value, axes, 0, 0, tiled=True)]
    all_to_all x5 -> x3, waiting for transfers between devices: 42.6 us -> 27.8 us  [exchange(): return lax.all_to_all(value, axes, 0, 0, tiled=True)]
    all_to_all x5 -> x3, starting transfers between devices: 26.9 us -> 16.8 us  [exchange(): return lax.all_to_all(value, axes, 0, 0, tiled=True)]
  transfers between devices with their start and end apart: 7 -> 5, of which waited for: 5 -> 3; matrix products, arithmetic and copies ran while one was open for 4% -> 3% of each run, Pallas kernels for 1% -> 2%
where the time goes in v7:
time: 143 us; the launch traced here: 142 us
  blocking collectives  70.1 us (49%)
  waiting for transfers between devices  27.8 us (19%)
  starting transfers between devices  16.9 us (12%)
  between operations  14.1 us (10%)
  Pallas kernels  8.31 us (6%)
  matrix products  3.09 us (2%)
  local copies, waits for them, and re-layouts  1.44 us (1%)
    all_to_all x3, blocking collectives, exchange(): return lax.all_to_all(value, axes, 0, 0, tiled=True)  70.1 us
    all_to_all x3, waiting for transfers between devices, exchange(): return lax.all_to_all(value, axes, 0, 0, tiled=True)  27.8 us
    all_to_all x3, starting transfers between devices, exchange(): return lax.all_to_all(value, axes, 0, 0, tiled=True)  16.8 us
    pallas_call x1, Pallas kernels, term_of(): pl.pallas_call(functools.partial(term_kernel, inv_tokens), out_shape=jax....  4.51 us
    dot_general x1, matrix products, on_device(): lax.dot_general(cotangent, weight, (((1,), (1,)), ((), ())), preferred_el...  3.09 us
  transfers between devices with their start and end apart: 5, of which 3 were waited for; matrix products, arithmetic and copies ran while one was open for 3% of the time, Pallas kernels for 2%

profile of v7, /device:TPU:1, one launch (start us, length us, event | category | flops | bytes accessed | tf_op | source)
XLA Modules:
  0.0 142.5 jit_solution(7518013997002555301)
XLA Ops:
  7.2 0.0 reduce-scatter.2.cloned.1.call-start
  7.2 4.5 %term.1 = f32[64,8,1664]{2,1,0:T(8,128)} custom-call(bf16[192,256]{1,0:T(8,128)(2,1)} %context_ref, bf16[192,4096]{1,0:T(8,128)(2,1)} %cotangent_hbm.1, f32[1,4]{1,0:T(1,128)} %bitcast.16), custom_call_target="tpu_custom_call" | custom-call | flops 402653184 | bytes 5767168 | tf_op jit(solution)/shard_map/term/pallas_call | solution.py:74
  11.7 0.0 copy-start.3
  11.7 0.0 copy-start
  11.7 0.0 copy-start.1
  11.8 0.0 reduce-scatter.2.cloned.1.call-update
  11.8 0.0 all-gather.2.cloned.1.call-start
  11.8 1.3 copy-done.3
  13.2 0.0 copy-done
  13.2 0.0 copy-done.1
  13.2 0.6 aside.1
  13.8 43.5 %all_to_all.30.value_ref = bf16[8,8,16,640]{3,2,1,0:T(8,128)(2,1)S(1)} all-to-all(bf16[8,8,16,640]{3,2,1,0:T(8,128)(2,1)S(1)} %aside.1), channel_id=1, replica_groups=mesh['y'=8,'z'=8,'x'=4,'c'=2] {'z'}, dimensions={0} | all-to-all | bytes 2621440 | tf_op jit(solution)/shard_map/all_to_all | solution.py:283
  57.3 0.0 copy-start.4
  57.3 0.7 arrival.1
  58.0 14.5 %all_to_all.31.aside_ref = f32[8,8,512]{2,1,0:T(8,128)S(1)} all-to-all(f32[8,8,512]{2,1,0:T(8,128)S(1)} %get-tuple-element.23), channel_id=1, replica_groups=mesh['y'=8,'z'=8,'x'=4,'c'=2] {'y'}, dimensions={0} | all-to-all | bytes 262144 | tf_op jit(solution)/shard_map/all_to_all | solution.py:283
  72.6 0.0 all-gather.2.cloned.1.call-update
  72.6 5.2 %all-to-all-start.2 = ((f32[8,8,1664]{2,1,0:T(8,128)}), f32[8,8,1664]{2,1,0:T(8,128)S(1)}, u32[]{:S(2)}, u32[]{:S(2)}) async-start(f32[8,8,1664]{2,1,0:T(8,128)} %bitcast.15), calls=%async_computation.3 | async-start | bytes 851968 | tf_op jit(solution)/shard_map/all_to_all | solution.py:283
  77.8 0.0 copy-done.4
  77.8 0.1 copy.11.state_ref
  77.9 12.7 %all-to-all-done.2.pieces_ref = f32[8,8,1664]{2,1,0:T(8,128)S(1)} async-done(((f32[8,8,1664]{2,1,0:T(8,128)}), f32[8,8,1664]{2,1,0:T(8,128)S(1)}, u32[]{:S(2)}, u32[]{:S(2)}) %all-to-all-start.2) | async-done | bytes 426016 | tf_op jit(solution)/shard_map/all_to_all | solution.py:283
  90.5 0.2 sums.1
  90.8 12.1 %all_to_all.32.value_ref = f32[8,16,128]{2,1,0:T(8,128)S(1)} all-to-all(f32[8,16,128]{2,1,0:T(8,128)S(1)} %get-tuple-element.26), channel_id=1, replica_groups=mesh['y'=8,'z'=8,'x'=4,'c'=2] {'x','c'}, dimensions={0} | all-to-all | bytes 131072 | tf_op jit(solution)/shard_map/all_to_all | solution.py:283
  102.9 0.7 split_fold.1
  103.6 5.7 %all-to-all-start.4 = ((f32[64,8,128]{2,1,0:T(8,128)}), f32[64,8,128]{2,1,0:T(8,128)S(1)}, u32[]{:S(2)}, u32[]{:S(2)}) async-start(f32[64,8,128]{2,1,0:T(8,128)} %get-tuple-element.27), calls=%async_computation.5 | async-start | bytes 524288 | tf_op jit(solution)/shard_map/all_to_all | solution.py:283
  109.3 0.6 reduce
  109.9 13.5 %all-to-all-done.4.value_ref = f32[64,8,128]{2,1,0:T(8,128)S(1)} async-done(((f32[64,8,128]{2,1,0:T(8,128)}), f32[64,8,128]{2,1,0:T(8,128)S(1)}, u32[]{:S(2)}, u32[]{:S(2)}) %all-to-all-start.4) | async-done | bytes 262176 | tf_op jit(solution)/shard_map/all_to_all | solution.py:283
  123.4 0.7 fold.1
  124.1 6.0 %all-to-all-start.5 = ((f32[8,8,128]{2,1,0:T(8,128)}), f32[8,8,128]{2,1,0:T(8,128)S(1)}, u32[]{:S(2)}, u32[]{:S(2)}) async-start(f32[8,8,128]{2,1,0:T(8,128)} %fold.1), calls=%async_computation.6 | async-start | bytes 65536 | tf_op jit(solution)/shard_map/all_to_all | solution.py:283
  130.1 3.1 %fusion = bf16[192,256]{1,0:T(8,128)(2,1)} fusion(bf16[256,4096]{1,0:T(8,128)(2,1)} %all-gather.2.cloned.1.call-done, bf16[192,4096]{1,0:T(8,128)(2,1)S(1)} %copy-done.3), kind=kOutput, calls=%fused_computation.1 | convolution fusion | flops 402702336 | bytes 3768320 | tf_op jit(solution)/shard_map/dot_general | solution.py:303
  133.2 1.6 %all-to-all-done.5 = f32[8,8,128]{2,1,0:T(8,128)S(1)} async-done(((f32[8,8,128]{2,1,0:T(8,128)}), f32[8,8,128]{2,1,0:T(8,128)S(1)}, u32[]{:S(2)}, u32[]{:S(2)}) %all-to-all-start.5) | async-done | bytes 32800 | tf_op jit(solution)/shard_map/all_to_all | solution.py:283
  134.8 0.0 copy-done.2
  134.8 0.8 update.1
  (4 shorter events, 0.0 us)
Async XLA Ops:
  7.2 65.4 %reduce-scatter.2.cloned.1.call-start = ((), (), s32[]{:S(2)}) async-start(), calls=%async_computation.7 | async-start | bytes 3833856 | tf_op jit(solution)/shard_map/reduce_scatter | solution.py:294
  11.7 1.4 copy-start.3
  11.7 1.4 %copy-start = (bf16[192,256]{1,0:T(8,128)(2,1)S(1)}, bf16[192,256]{1,0:T(8,128)(2,1)}, u32[]{:S(2)}) copy-start(bf16[192,256]{1,0:T(8,128)(2,1)} %context_ref) | copy-start | bytes 294916
  11.7 1.4 %copy-start.1 = (f32[4,4096]{1,0:T(4,128)S(1)}, f32[4,4096]{1,0:T(4,128)}, u32[]{:S(2)}) copy-start(f32[4,4096]{1,0:T(4,128)} %weight_ref.1) | copy-start | bytes 196612
  11.8 118.3 %all-gather.2.cloned.1.call-start = ((), (), s32[]{:S(2)}) async-start(), calls=%async_computation.8 | async-start | bytes 2359296 | tf_op jit(solution)/shard_map/all_gather | solution.py:302
  57.3 20.5 %copy-start.4 = (f32[4]{0:T(128)S(1)}, f32[4]{0:T(128)}, u32[]{:S(2)}) copy-start(f32[4]{0:T(128)} %param.8) | copy-start | bytes 52
  72.6 17.9 %all-to-all-start.2 = ((f32[8,8,1664]{2,1,0:T(8,128)}), f32[8,8,1664]{2,1,0:T(8,128)S(1)}, u32[]{:S(2)}, u32[]{:S(2)}) async-start(f32[8,8,1664]{2,1,0:T(8,128)} %bitcast.15), calls=%async_computation.3 | async-start | bytes 851968 | tf_op jit(solution)/shard_map/all_to_all | solution.py:283
  103.6 19.8 %all-to-all-start.4 = ((f32[64,8,128]{2,1,0:T(8,128)}), f32[64,8,128]{2,1,0:T(8,128)S(1)}, u32[]{:S(2)}, u32[]{:S(2)}) async-start(f32[64,8,128]{2,1,0:T(8,128)} %get-tuple-element.27), calls=%async_computation.5 | async-start | bytes 524288 | tf_op jit(solution)/shard_map/all_to_all | solution.py:283
  124.1 10.7 %all-to-all-start.5 = ((f32[8,8,128]{2,1,0:T(8,128)}), f32[8,8,128]{2,1,0:T(8,128)S(1)}, u32[]{:S(2)}, u32[]{:S(2)}) async-start(f32[8,8,128]{2,1,0:T(8,128)} %fold.1), calls=%async_computation.6 | async-start | bytes 65536 | tf_op jit(solution)/shard_map/all_to_all | solution.py:283
  130.1 4.7 %copy-start.2 = (f32[4096]{0:T(1024)S(1)}, f32[4096]{0:T(1024)}, u32[]{:S(2)}) copy-start(f32[4096]{0:T(1024)} %param.9) | copy-start | bytes 49156
Sparse Core Ops, SparseCore 0:
  11.9 55.4 reduce-scatter.1
  72.7 39.8 all-gather.1

commit v8 on v7

--- a/solution.py
+++ b/solution.py
@@ -10,7 +10,7 @@
 BETA = 0.8
 EPS1 = 1e-30
 CLIP = 1.0
-CHUNK = 512
+CHUNK = 768
 ASIDE = 512
 LANES = 128
 NEAR = ("x", "c")
@@ -23,14 +23,12 @@
     return [(i, min(CHUNK, stop - i)) for i in range(start, stop, CHUNK)]
 
 
-def product(context_ref, cotangent, inv_tokens):
-    return inv_tokens * lax.dot_general(
-        context_ref[...], cotangent, (((0,), (0,)), ((), ())), preferred_element_type=jnp.float32
-    )
-
-
-def term_kernel(inv_tokens, context_hbm, cotangent_hbm, state_ref, out_hbm, context_ref, cotangent_ref, out_ref, in_sems, out_sems):
-    peers, rows, width = out_ref.shape[0], out_ref.shape[1] // 2, out_ref.shape[2] - LANES
+def product(context, cotangent, inv_tokens):
+    return inv_tokens * jnp.dot(context, cotangent, preferred_element_type=jnp.float32)
+
+
+def term_kernel(inv_tokens, context_hbm, cotangent_hbm, out_hbm, context_ref, cotangent_ref, out_ref, in_sems, out_sems):
+    peers, rows, width = out_ref.shape[0], out_ref.shape[1] // 2, out_ref.shape[2]
     half_cols = cotangent_hbm.shape[1] // 2
     first = pltpu.make_async_copy(context_hbm, context_ref, in_sems.at[0])
     first.start()
@@ -44,19 +42,16 @@
             copy.start()
             loads.append(copy)
     first.wait()
+    context = context_ref[...].T
     stores = []
     for k, (start, size) in enumerate(spans(0, width)):
         for half in range(2):
             loads[2 * k + half].wait()
             place = half * half_cols + start
-            term = product(context_ref, cotangent_ref[:, place:place + size], inv_tokens)
+            term = product(context, cotangent_ref[:, place:place + size], inv_tokens)
             out_ref[:, half * rows:(half + 1) * rows, start:start + size] = term.reshape(
                 peers, rows, size
             )
-        if start + size == width:
-            total = jnp.sum(state_ref[...], axis=1, keepdims=True).reshape(1, 1, 1)
-            out_ref[:, :, width:] = jnp.broadcast_to(total, (peers, 2 * rows, LANES))
-            size += LANES
         place = pl.ds(start, size)
         copy = pltpu.make_async_copy(
             out_ref.at[:, :, place], out_hbm.at[:, :, place], out_sems.at[k]
@@ -67,14 +62,14 @@
         copy.wait()
 
 
-def term_of(context, cotangent, row_state, inv_tokens, peers, rows):
+def term_of(context, cotangent, inv_tokens, peers, rows):
     tokens, cols = cotangent.shape
-    width = cols // 2 - ASIDE + LANES
-    count = len(spans(0, width - LANES))
+    width = cols // 2 - ASIDE
+    count = len(spans(0, width))
     return pl.pallas_call(
         functools.partial(term_kernel, inv_tokens),
         out_shape=jax.ShapeDtypeStruct((peers, 2 * rows, width), jnp.float32),
-        in_specs=[pl.BlockSpec(memory_space=pl.ANY)] * 2 + [VMEM],
+        in_specs=[pl.BlockSpec(memory_space=pl.ANY)] * 2,
         out_specs=pl.BlockSpec(memory_space=pl.ANY),
         scratch_shapes=[
             pltpu.VMEM(context.shape, context.dtype),
@@ -90,14 +85,15 @@
             transcendentals=0,
         ),
         name="term",
-    )(context, cotangent, row_state[None])
+    )(context, cotangent)
 
 
 def aside_kernel(inv_tokens, context_ref, left_ref, right_ref, weight_ref, out_ref, term_ref):
     nz, ny, rows, _ = term_ref.shape
     rows //= 2
+    context = context_ref[...].T
     for half, cotangent_ref in enumerate((left_ref, right_ref)):
-        term = product(context_ref, cotangent_ref[...], inv_tokens)
+        term = product(context, cotangent_ref[...], inv_tokens)
         for y in range(ny):
             part = term[y * nz * rows:(y + 1) * nz * rows]
             term_ref[:, y, half * rows:(half + 1) * rows, :] = part.reshape(nz, rows, ASIDE)
@@ -165,12 +161,14 @@
 
 
 def sums_kernel(pieces_ref, aside_ref, state_ref, grad_ref, row_ref, packed_ref):
-    most = jnp.sum(pieces_ref[...], axis=0)
-    width = most.shape[1] - LANES
-    grad = jnp.concatenate([most[:, :width], jnp.sum(aside_ref[...], axis=0)], axis=1)
+    grad = jnp.concatenate(
+        [jnp.sum(pieces_ref[...], axis=0), jnp.sum(aside_ref[...], axis=0)], axis=1
+    )
     grad_ref[...] = grad
-    lines = packed_ref.shape[1] // 2
-    packed_ref[:, lines:, :] = jnp.broadcast_to(most[None, :lines, width:], (packed_ref.shape[0], lines, LANES))
+    peers, _, size = packed_ref.shape
+    lines = size // LANES - 1
+    state_sum = jnp.sum(state_ref[...], axis=0, keepdims=True).reshape(1, 1, 1)
+    packed_ref[:, :, lines * LANES:] = jnp.broadcast_to(state_sum, (peers, 1, LANES))
     rows = grad.shape[0] // 2
     plain = grad * grad
     squared = plain + EPS1
@@ -185,17 +183,17 @@
             for i in range(per_half):
                 place = (2 * which + half) * per_half + i
                 group, line = divmod(place, lines)
-                packed_ref[group, line:line + 1, :] = total[:, i * LANES:(i + 1) * LANES]
+                packed_ref[group, :, line * LANES:(line + 1) * LANES] = total[:, i * LANES:(i + 1) * LANES]
 
 
 def sums_of(pieces, aside, row_state, peers):
-    rows, cols = pieces.shape[1], pieces.shape[2] - LANES + ASIDE
+    rows, cols = pieces.shape[1], pieces.shape[2] + ASIDE
     return pl.pallas_call(
         sums_kernel,
         out_shape=(
             jax.ShapeDtypeStruct((rows, cols), jnp.float32),
             jax.ShapeDtypeStruct(row_state.shape, jnp.float32),
-            jax.ShapeDtypeStruct((peers, 2 * 4 * cols // (peers * LANES), LANES), jnp.float32),
+            jax.ShapeDtypeStruct((peers, 1, 4 * cols // peers + LANES), jnp.float32),
         ),
         in_specs=[VMEM] * 3,
         out_specs=(VMEM,) * 3,
@@ -257,28 +255,6 @@
     )(value)
 
 
-def split_kernel(value_ref, out_ref, rest_ref):
-    total = jnp.sum(value_ref[...], axis=0, keepdims=True)
-    lines = out_ref.shape[1]
-    out_ref[...] = jnp.broadcast_to(total[:, :lines], out_ref.shape)
-    rest_ref[...] = total[0, lines:]
-
-
-def split_fold(value, copies):
-    lines = value.shape[1] // 2
-    return pl.pallas_call(
-        split_kernel,
-        out_shape=(
-            jax.ShapeDtypeStruct((copies, lines, LANES), value.dtype),
-            jax.ShapeDtypeStruct((lines, LANES), value.dtype),
-        ),
-        in_specs=[VMEM],
-        out_specs=(VMEM,) * 2,
-        compiler_params=PARAMS,
-        name="split_fold",
-    )(value)
-
-
 def exchange(value, axes):
     return lax.all_to_all(value, axes, 0, 0, tiled=True)
 
@@ -290,7 +266,7 @@
     inv_tokens = 1.0 / (cotangent.shape[0] * ny * nz)
     entries = rows * ny * nz * nmp * cols
 
-    term = term_of(context, cotangent, row_state, inv_tokens, ny * nz, rows)
+    term = term_of(context, cotangent, inv_tokens, ny * nz, rows)
     part = lax.psum_scatter(
         term.reshape(ny * nz * 2 * rows, term.shape[2]), "y", scatter_dimension=0, tiled=True
     )
@@ -306,9 +282,11 @@
 
     pieces = exchange(part.reshape(nz, 2 * rows, term.shape[2]), "z")
     grad, row_new, packed = sums_of(pieces, aside, row_state[:, None], nmp)
-    packed, state_sum = split_fold(exchange(packed, NEAR), ny * nz)
+    packed = fold(exchange(packed, NEAR), ny * nz)
     packed = fold(exchange(packed, FAR), nmp)
-    packed = exchange(packed, NEAR).reshape(2 * cols // LANES, LANES)
+    state_sum = packed[0, :, packed.shape[2] - LANES:]
+    packed = exchange(packed[:, :, :packed.shape[2] - LANES], NEAR)
+    packed = packed.reshape(2 * cols // LANES, LANES)
     packed, grad_input = lax.optimization_barrier((packed, grad_input))
     update, col_new, update_rms = update_of(
         packed, state_sum, grad, row_new, col_state.reshape(cols // LANES, LANES), entries

time: 143 us -> 140 us (0.979)
  waiting for transfers between devices: 27.8 us -> 25.7 us
  starting transfers between devices: 16.9 us -> 15 us
  blocking collectives: 70.1 us -> 71.9 us
  Pallas kernels: 8.31 us -> 6.82 us
    all_to_all x3, waiting for transfers between devices: 27.8 us -> 25.7 us  [exchange(): return lax.all_to_all(value, axes, 0, 0, tiled=True)]
    all_to_all x3, starting transfers between devices: 16.8 us -> 14.9 us  [exchange(): return lax.all_to_all(value, axes, 0, 0, tiled=True)]
    all_to_all x3, blocking collectives: 70.1 us -> 71.9 us  [exchange(): return lax.all_to_all(value, axes, 0, 0, tiled=True)]
where the time goes in v8:
time: 140 us; the launch traced here: 139 us
  blocking collectives  71.9 us (51%)
  waiting for transfers between devices  25.7 us (18%)
  starting transfers between devices  15 us (11%)
  between operations  14.1 us (10%)
  Pallas kernels  6.82 us (5%)
  matrix products  3.08 us (2%)
  local copies, waits for them, and re-layouts  2.06 us (1%)
    all_to_all x3, blocking collectives, exchange(): return lax.all_to_all(value, axes, 0, 0, tiled=True)  71.9 us
    all_to_all x3, waiting for transfers between devices, exchange(): return lax.all_to_all(value, axes, 0, 0, tiled=True)  25.7 us
    all_to_all x3, starting transfers between devices, exchange(): return lax.all_to_all(value, axes, 0, 0, tiled=True)  14.9 us
    pallas_call x1, Pallas kernels, term_of(): pl.pallas_call(functools.partial(term_kernel, inv_tokens), out_shape=jax....  3.42 us
    dot_general x1, matrix products, on_device(): lax.dot_general(cotangent, weight, (((1,), (1,)), ((), ())), preferred_el...  3.08 us
  transfers between devices with their start and end apart: 5, of which 3 were waited for; matrix products, arithmetic and copies ran while one was open for 3% of the time, Pallas kernels for 2%

profile of v8, /device:TPU:1, one launch (start us, length us, event | category | flops | bytes accessed | tf_op | source)
XLA Modules:
  0.0 139.3 jit_solution(10429132995725625443)
XLA Ops:
  7.2 0.0 reduce-scatter.2.cloned.1.call-start
  7.2 3.4 %term.1 = f32[64,8,1536]{2,1,0:T(8,128)} custom-call(bf16[192,256]{1,0:T(8,128)(2,1)} %context_ref, bf16[192,4096]{1,0:T(8,128)(2,1)} %cotangent_hbm.1), custom_call_target="tpu_custom_call" | custom-call | flops 402653184 | bytes 5767168 | tf_op jit(solution)/shard_map/term/pallas_call | solution.py:69
  10.6 0.0 copy-start.3
  10.6 0.0 copy-start
  10.7 0.0 copy-start.1
  10.7 0.0 reduce-scatter.2.cloned.1.call-update
  10.7 0.0 all-gather.2.cloned.1.call-start
  10.7 1.3 copy-done.3
  12.1 0.0 copy-done
  12.1 0.0 copy-done.1
  12.1 0.6 aside.1
  12.7 43.5 %all_to_all.30.value_ref = bf16[8,8,16,640]{3,2,1,0:T(8,128)(2,1)S(1)} all-to-all(bf16[8,8,16,640]{3,2,1,0:T(8,128)(2,1)S(1)} %aside.1), channel_id=1, replica_groups=mesh['y'=8,'z'=8,'x'=4,'c'=2] {'z'}, dimensions={0} | all-to-all | bytes 2621440 | tf_op jit(solution)/shard_map/all_to_all | solution.py:259
  56.2 0.7 arrival.1
  57.0 14.5 %all_to_all.31.aside_ref = f32[8,8,512]{2,1,0:T(8,128)S(1)} all-to-all(f32[8,8,512]{2,1,0:T(8,128)S(1)} %get-tuple-element.21), channel_id=1, replica_groups=mesh['y'=8,'z'=8,'x'=4,'c'=2] {'y'}, dimensions={0} | all-to-all | bytes 262144 | tf_op jit(solution)/shard_map/all_to_all | solution.py:259
  71.5 0.0 all-gather.2.cloned.1.call-update
  71.5 3.5 %all-to-all-start.2 = ((f32[8,8,1536]{2,1,0:T(8,128)}), f32[8,8,1536]{2,1,0:T(8,128)S(1)}, u32[]{:S(2)}, u32[]{:S(2)}) async-start(f32[8,8,1536]{2,1,0:T(8,128)} %bitcast.16), calls=%async_computation.3 | async-start | bytes 786432 | tf_op jit(solution)/shard_map/all_to_all | solution.py:259
  75.0 0.0 copy-done.4
  75.0 0.1 copy.11.state_ref
  75.1 10.7 %all-to-all-done.2.pieces_ref = f32[8,8,1536]{2,1,0:T(8,128)S(1)} async-done(((f32[8,8,1536]{2,1,0:T(8,128)}), f32[8,8,1536]{2,1,0:T(8,128)S(1)}, u32[]{:S(2)}, u32[]{:S(2)}) %all-to-all-start.2) | async-done | bytes 393248 | tf_op jit(solution)/shard_map/all_to_all | solution.py:259
  85.7 0.2 sums.1
  86.0 13.8 %all_to_all.32.value_ref = f32[8,1,1152]{2,1,0:T(1,128)S(1)} all-to-all(f32[8,1,1152]{2,1,0:T(1,128)S(1)} %get-tuple-element.24), channel_id=1, replica_groups=mesh['y'=8,'z'=8,'x'=4,'c'=2] {'x','c'}, dimensions={0} | all-to-all | bytes 73728 | tf_op jit(solution)/shard_map/all_to_all | solution.py:259
  99.8 0.8 fold.2
  100.6 4.6 %all-to-all-start.4 = ((f32[64,1,1152]{2,1,0:T(1,128)}), f32[64,1,1152]{2,1,0:T(1,128)S(1)}, u32[]{:S(2)}, u32[]{:S(2)}) async-start(f32[64,1,1152]{2,1,0:T(1,128)} %fold.2), calls=%async_computation.5 | async-start | bytes 589824 | tf_op jit(solution)/shard_map/all_to_all | solution.py:259
  105.2 0.6 reduce
  105.9 13.4 %all-to-all-done.4.value_ref = f32[64,1,1152]{2,1,0:T(1,128)S(1)} async-done(((f32[64,1,1152]{2,1,0:T(1,128)}), f32[64,1,1152]{2,1,0:T(1,128)S(1)}, u32[]{:S(2)}, u32[]{:S(2)}) %all-to-all-start.4) | async-done | bytes 294944 | tf_op jit(solution)/shard_map/all_to_all | solution.py:259
  119.3 0.2 fold.3
  119.5 0.6 slice.16
  120.1 6.8 %all-to-all-start.5 = ((f32[8,1,1024]{2,1,0:T(1,128)}), f32[8,1,1024]{2,1,0:T(1,128)S(1)}, u32[]{:S(2)}, u32[]{:S(2)}) async-start(f32[8,1,1024]{2,1,0:T(1,128)} %slice.16), calls=%async_computation.6 | async-start | bytes 65536 | tf_op jit(solution)/shard_map/all_to_all | solution.py:259
  126.9 0.0 all-gather.2.cloned.1.call-done
  126.9 3.1 %fusion = bf16[192,256]{1,0:T(8,128)(2,1)} fusion(bf16[256,4096]{1,0:T(8,128)(2,1)} %all-gather.2.cloned.1.call-done, bf16[192,4096]{1,0:T(8,128)(2,1)S(1)} %copy-done.3), kind=kOutput, calls=%fused_computation.1 | convolution fusion | flops 402702336 | bytes 3768320 | tf_op jit(solution)/shard_map/dot_general | solution.py:279
  130.0 1.6 %all-to-all-done.5 = f32[8,1,1024]{2,1,0:T(1,128)S(1)} async-done(((f32[8,1,1024]{2,1,0:T(1,128)}), f32[8,1,1024]{2,1,0:T(1,128)S(1)}, u32[]{:S(2)}, u32[]{:S(2)}) %all-to-all-start.5) | async-done | bytes 32800 | tf_op jit(solution)/shard_map/all_to_all | solution.py:259
  131.6 0.9 update.1
  (6 shorter events, 0.0 us)
Async XLA Ops:
  7.2 64.3 %reduce-scatter.2.cloned.1.call-start = ((), (), s32[]{:S(2)}) async-start(), calls=%async_computation.7 | async-start | bytes 3538944 | tf_op jit(solution)/shard_map/reduce_scatter | solution.py:270
  10.6 1.4 %copy-start.3 = (bf16[192,4096]{1,0:T(8,128)(2,1)S(1)}, bf16[192,4096]{1,0:T(8,128)(2,1)}, u32[]{:S(2)}) copy-start(bf16[192,4096]{1,0:T(8,128)(2,1)} %cotangent_hbm.1) | copy-start | bytes 4718596
  10.6 1.4 %copy-start = (bf16[192,256]{1,0:T(8,128)(2,1)S(1)}, bf16[192,256]{1,0:T(8,128)(2,1)}, u32[]{:S(2)}) copy-start(bf16[192,256]{1,0:T(8,128)(2,1)} %context_ref) | copy-start | bytes 294916
  10.7 1.4 %copy-start.1 = (f32[4,4096]{1,0:T(4,128)S(1)}, f32[4,4096]{1,0:T(4,128)}, u32[]{:S(2)}) copy-start(f32[4,4096]{1,0:T(4,128)} %weight_ref.1) | copy-start | bytes 196612
  10.7 116.2 %all-gather.2.cloned.1.call-start = ((), (), s32[]{:S(2)}) async-start(), calls=%async_computation.8 | async-start | bytes 2359296 | tf_op jit(solution)/shard_map/all_gather | solution.py:278
  56.2 18.8 %copy-start.4 = (f32[4]{0:T(128)S(1)}, f32[4]{0:T(128)}, u32[]{:S(2)}) copy-start(f32[4]{0:T(128)} %param.8) | copy-start | bytes 52
  71.5 14.2 %all-to-all-start.2 = ((f32[8,8,1536]{2,1,0:T(8,128)}), f32[8,8,1536]{2,1,0:T(8,128)S(1)}, u32[]{:S(2)}, u32[]{:S(2)}) async-start(f32[8,8,1536]{2,1,0:T(8,128)} %bitcast.16), calls=%async_computation.3 | async-start | bytes 786432 | tf_op jit(solution)/shard_map/all_to_all | solution.py:259
  100.6 18.7 %all-to-all-start.4 = ((f32[64,1,1152]{2,1,0:T(1,128)}), f32[64,1,1152]{2,1,0:T(1,128)S(1)}, u32[]{:S(2)}, u32[]{:S(2)}) async-start(f32[64,1,1152]{2,1,0:T(1,128)} %fold.2), calls=%async_computation.5 | async-start | bytes 589824 | tf_op jit(solution)/shard_map/all_to_all | solution.py:259
  120.1 11.5 %all-to-all-start.5 = ((f32[8,1,1024]{2,1,0:T(1,128)}), f32[8,1,1024]{2,1,0:T(1,128)S(1)}, u32[]{:S(2)}, u32[]{:S(2)}) async-start(f32[8,1,1024]{2,1,0:T(1,128)} %slice.16), calls=%async_computation.6 | async-start | bytes 65536 | tf_op jit(solution)/shard_map/all_to_all | solution.py:259
  126.9 4.7 %copy-start.2 = (f32[4096]{0:T(1024)S(1)}, f32[4096]{0:T(1024)}, u32[]{:S(2)}) copy-start(f32[4096]{0:T(1024)} %param.9) | copy-start | bytes 49156
Sparse Core Ops, SparseCore 0:
  10.8 51.8 reduce-scatter.1
  71.6 38.9 all-gather.1

commit v9 on v8

--- a/solution.py
+++ b/solution.py
@@ -14,7 +14,6 @@
 ASIDE = 512
 LANES = 128
 NEAR = ("x", "c")
-FAR = ("y", "z")
 VMEM = pl.BlockSpec(memory_space=pltpu.VMEM)
 PARAMS = pltpu.CompilerParams(vmem_limit_bytes=32 * 2**20)
 
@@ -255,6 +254,28 @@
     )(value)
 
 
+def split_kernel(value_ref, out_ref, last_ref):
+    total = jnp.sum(value_ref[...], axis=0, keepdims=True)
+    size = out_ref.shape[2]
+    out_ref[...] = jnp.broadcast_to(total[:, :, :size], out_ref.shape)
+    last_ref[...] = total[0, :, size:]
+
+
+def split_fold(value, copies):
+    size = value.shape[2] - LANES
+    return pl.pallas_call(
+        split_kernel,
+        out_shape=(
+            jax.ShapeDtypeStruct((copies, 1, size), value.dtype),
+            jax.ShapeDtypeStruct((1, LANES), value.dtype),
+        ),
+        in_specs=[VMEM],
+        out_specs=(VMEM,) * 2,
+        compiler_params=PARAMS,
+        name="split_fold",
+    )(value)
+
+
 def exchange(value, axes):
     return lax.all_to_all(value, axes, 0, 0, tiled=True)
 
@@ -282,11 +303,10 @@
 
     pieces = exchange(part.reshape(nz, 2 * rows, term.shape[2]), "z")
     grad, row_new, packed = sums_of(pieces, aside, row_state[:, None], nmp)
-    packed = fold(exchange(packed, NEAR), ny * nz)
-    packed = fold(exchange(packed, FAR), nmp)
-    state_sum = packed[0, :, packed.shape[2] - LANES:]
-    packed = exchange(packed[:, :, :packed.shape[2] - LANES], NEAR)
-    packed = packed.reshape(2 * cols // LANES, LANES)
+    packed = fold(exchange(packed, NEAR), nz)
+    packed = fold(exchange(packed, "z"), ny)
+    packed, state_sum = split_fold(exchange(packed, "y"), nmp)
+    packed = exchange(packed, NEAR).reshape(2 * cols // LANES, LANES)
     packed, grad_input = lax.optimization_barrier((packed, grad_input))
     update, col_new, update_rms = update_of(
         packed, state_sum, grad, row_new, col_state.reshape(cols // LANES, LANES), entries

time: 140 us -> 140 us (level)
  blocking collectives: 71.9 us -> 81.3 us
  waiting for transfers between devices: 25.7 us -> 18.5 us
  starting transfers between devices: 15 us -> 13 us
    all_to_all x3 -> x4, blocking collectives: 71.9 us -> 81.3 us  [exchange(): return lax.all_to_all(value, axes, 0, 0, tiled=True)]
    all_to_all x3, waiting for transfers between devices: 25.7 us -> 18.5 us  [exchange(): return lax.all_to_all(value, axes, 0, 0, tiled=True)]
    all_to_all x3, starting transfers between devices: 14.9 us -> 12.9 us  [exchange(): return lax.all_to_all(value, axes, 0, 0, tiled=True)]
where the time goes in v9:
time: 140 us; the launch traced here: 139 us
  blocking collectives  81.3 us (58%)
  waiting for transfers between devices  18.5 us (13%)
  between operations  14.1 us (10%)
  starting transfers between devices  13 us (9%)
  Pallas kernels  7.18 us (5%)
  matrix products  3.09 us (2%)
  local copies, waits for them, and re-layouts  1.44 us (1%)
    all_to_all x4, blocking collectives, exchange(): return lax.all_to_all(value, axes, 0, 0, tiled=True)  81.3 us
    all_to_all x3, waiting for transfers between devices, exchange(): return lax.all_to_all(value, axes, 0, 0, tiled=True)  18.5 us
    all_to_all x3, starting transfers between devices, exchange(): return lax.all_to_all(value, axes, 0, 0, tiled=True)  12.9 us
    pallas_call x1, Pallas kernels, term_of(): pl.pallas_call(functools.partial(term_kernel, inv_tokens), out_shape=jax....  3.44 us
    dot_general x1, matrix products, on_device(): lax.dot_general(cotangent, weight, (((1,), (1,)), ((), ())), preferred_el...  3.09 us
  transfers between devices with their start and end apart: 5, of which 3 were waited for; matrix products, arithmetic and copies ran while one was open for 3% of the time, Pallas kernels for 2%

profile of v9, /device:TPU:1, one launch (start us, length us, event | category | flops | bytes accessed | tf_op | source)
XLA Modules:
  0.0 139.3 jit_solution(2713609954662709510)
XLA Ops:
  7.2 0.0 reduce-scatter.2.cloned.1.call-start
  7.2 3.4 %term.1 = f32[64,8,1536]{2,1,0:T(8,128)} custom-call(bf16[192,256]{1,0:T(8,128)(2,1)} %context_ref, bf16[192,4096]{1,0:T(8,128)(2,1)} %cotangent_hbm.1), custom_call_target="tpu_custom_call" | custom-call | flops 402653184 | bytes 5767168 | tf_op jit(solution)/shard_map/term/pallas_call | solution.py:68
  10.7 0.0 copy-start.3
  10.7 0.0 copy-start
  10.7 0.0 copy-start.1
  10.7 0.0 reduce-scatter.2.cloned.1.call-update
  10.7 0.0 all-gather.2.cloned.1.call-start
  10.8 1.3 copy-done.3
  12.1 0.0 copy-done
  12.1 0.0 copy-done.1
  12.1 0.6 aside.1
  12.7 43.5 %all_to_all.35.value_ref = bf16[8,8,16,640]{3,2,1,0:T(8,128)(2,1)S(1)} all-to-all(bf16[8,8,16,640]{3,2,1,0:T(8,128)(2,1)S(1)} %aside.1), channel_id=1, replica_groups=mesh['y'=8,'z'=8,'x'=4,'c'=2] {'z'}, dimensions={0} | all-to-all | bytes 2621440 | tf_op jit(solution)/shard_map/all_to_all | solution.py:280
  56.2 0.7 arrival.1
  57.0 14.5 %all_to_all.36.aside_ref = f32[8,8,512]{2,1,0:T(8,128)S(1)} all-to-all(f32[8,8,512]{2,1,0:T(8,128)S(1)} %get-tuple-element.23), channel_id=1, replica_groups=mesh['y'=8,'z'=8,'x'=4,'c'=2] {'y'}, dimensions={0} | all-to-all | bytes 262144 | tf_op jit(solution)/shard_map/all_to_all | solution.py:280
  71.5 0.0 all-gather.2.cloned.1.call-update
  71.5 3.5 %all-to-all-start.2 = ((f32[8,8,1536]{2,1,0:T(8,128)}), f32[8,8,1536]{2,1,0:T(8,128)S(1)}, u32[]{:S(2)}, u32[]{:S(2)}) async-start(f32[8,8,1536]{2,1,0:T(8,128)} %bitcast.14), calls=%async_computation.3 | async-start | bytes 786432 | tf_op jit(solution)/shard_map/all_to_all | solution.py:280
  75.0 0.0 copy-done.4
  75.0 0.1 copy.11.state_ref
  75.1 10.6 %all-to-all-done.2.pieces_ref = f32[8,8,1536]{2,1,0:T(8,128)S(1)} async-done(((f32[8,8,1536]{2,1,0:T(8,128)}), f32[8,8,1536]{2,1,0:T(8,128)S(1)}, u32[]{:S(2)}, u32[]{:S(2)}) %all-to-all-start.2) | async-done | bytes 393248 | tf_op jit(solution)/shard_map/all_to_all | solution.py:280
  85.8 0.2 sums.1
  86.0 13.9 %all_to_all.37.value_ref = f32[8,1,1152]{2,1,0:T(1,128)S(1)} all-to-all(f32[8,1,1152]{2,1,0:T(1,128)S(1)} %get-tuple-element.26), channel_id=1, replica_groups=mesh['y'=8,'z'=8,'x'=4,'c'=2] {'x','c'}, dimensions={0} | all-to-all | bytes 73728 | tf_op jit(solution)/shard_map/all_to_all | solution.py:280
  99.9 9.4 %all_to_all.38.value_ref = f32[8,1,1152]{2,1,0:T(1,128)S(1)} all-to-all(f32[8,1,1152]{2,1,0:T(1,128)S(1)} %fold.2), channel_id=1, replica_groups=mesh['y'=8,'z'=8,'x'=4,'c'=2] {'z'}, dimensions={0} | all-to-all | bytes 73728 | tf_op jit(solution)/shard_map/all_to_all | solution.py:280
  109.3 0.6 fold.3
  109.9 3.3 %all-to-all-start.5 = ((f32[8,1,1152]{2,1,0:T(1,128)}), f32[8,1,1152]{2,1,0:T(1,128)S(1)}, u32[]{:S(2)}, u32[]{:S(2)}) async-start(f32[8,1,1152]{2,1,0:T(1,128)} %fold.3), calls=%async_computation.6 | async-start | bytes 73728 | tf_op jit(solution)/shard_map/all_to_all | solution.py:280
  113.3 0.6 reduce
  113.9 6.2 %all-to-all-done.5.value_ref = f32[8,1,1152]{2,1,0:T(1,128)S(1)} async-done(((f32[8,1,1152]{2,1,0:T(1,128)}), f32[8,1,1152]{2,1,0:T(1,128)S(1)}, u32[]{:S(2)}, u32[]{:S(2)}) %all-to-all-start.5) | async-done | bytes 36896 | tf_op jit(solution)/shard_map/all_to_all | solution.py:280
  120.1 0.6 split_fold.1
  120.8 6.1 %all-to-all-start.6 = ((f32[8,1,1024]{2,1,0:T(1,128)}), f32[8,1,1024]{2,1,0:T(1,128)S(1)}, u32[]{:S(2)}, u32[]{:S(2)}) async-start(f32[8,1,1024]{2,1,0:T(1,128)} %get-tuple-element.27), calls=%async_computation.7 | async-start | bytes 65536 | tf_op jit(solution)/shard_map/all_to_all | solution.py:280
  126.9 3.1 %fusion = bf16[192,256]{1,0:T(8,128)(2,1)} fusion(bf16[256,4096]{1,0:T(8,128)(2,1)} %all-gather.2.cloned.1.call-done, bf16[192,4096]{1,0:T(8,128)(2,1)S(1)} %copy-done.3), kind=kOutput, calls=%fused_computation.1 | convolution fusion | flops 402702336 | bytes 3768320 | tf_op jit(solution)/shard_map/dot_general | solution.py:300
  130.0 1.6 %all-to-all-done.6 = f32[8,1,1024]{2,1,0:T(1,128)S(1)} async-done(((f32[8,1,1024]{2,1,0:T(1,128)}), f32[8,1,1024]{2,1,0:T(1,128)S(1)}, u32[]{:S(2)}, u32[]{:S(2)}) %all-to-all-start.6) | async-done | bytes 32800 | tf_op jit(solution)/shard_map/all_to_all | solution.py:280
  131.6 0.0 copy-done.2
  131.6 0.9 update.1
  (6 shorter events, 0.1 us)
Async XLA Ops:
  7.2 64.4 %reduce-scatter.2.cloned.1.call-start = ((), (), s32[]{:S(2)}) async-start(), calls=%async_computation.8 | async-start | bytes 3538944 | tf_op jit(solution)/shard_map/reduce_scatter | solution.py:291
  10.7 1.4 %copy-start.3 = (bf16[192,4096]{1,0:T(8,128)(2,1)S(1)}, bf16[192,4096]{1,0:T(8,128)(2,1)}, u32[]{:S(2)}) copy-start(bf16[192,4096]{1,0:T(8,128)(2,1)} %cotangent_hbm.1) | copy-start | bytes 4718596
  10.7 1.4 %copy-start = (bf16[192,256]{1,0:T(8,128)(2,1)S(1)}, bf16[192,256]{1,0:T(8,128)(2,1)}, u32[]{:S(2)}) copy-start(bf16[192,256]{1,0:T(8,128)(2,1)} %context_ref) | copy-start | bytes 294916
  10.7 1.4 %copy-start.1 = (f32[4,4096]{1,0:T(4,128)S(1)}, f32[4,4096]{1,0:T(4,128)}, u32[]{:S(2)}) copy-start(f32[4,4096]{1,0:T(4,128)} %weight_ref.1) | copy-start | bytes 196612
  10.7 116.2 %all-gather.2.cloned.1.call-start = ((), (), s32[]{:S(2)}) async-start(), calls=%async_computation.9 | async-start | bytes 2359296 | tf_op jit(solution)/shard_map/all_gather | solution.py:299
  56.2 18.8 %copy-start.4 = (f32[4]{0:T(128)S(1)}, f32[4]{0:T(128)}, u32[]{:S(2)}) copy-start(f32[4]{0:T(128)} %param.8) | copy-start | bytes 52
  71.5 14.2 %all-to-all-start.2 = ((f32[8,8,1536]{2,1,0:T(8,128)}), f32[8,8,1536]{2,1,0:T(8,128)S(1)}, u32[]{:S(2)}, u32[]{:S(2)}) async-start(f32[8,8,1536]{2,1,0:T(8,128)} %bitcast.14), calls=%async_computation.3 | async-start | bytes 786432 | tf_op jit(solution)/shard_map/all_to_all | solution.py:280
  109.9 10.2 %all-to-all-start.5 = ((f32[8,1,1152]{2,1,0:T(1,128)}), f32[8,1,1152]{2,1,0:T(1,128)S(1)}, u32[]{:S(2)}, u32[]{:S(2)}) async-start(f32[8,1,1152]{2,1,0:T(1,128)} %fold.3), calls=%async_computation.6 | async-start | bytes 73728 | tf_op jit(solution)/shard_map/all_to_all | solution.py:280
  120.8 10.9 %all-to-all-start.6 = ((f32[8,1,1024]{2,1,0:T(1,128)}), f32[8,1,1024]{2,1,0:T(1,128)S(1)}, u32[]{:S(2)}, u32[]{:S(2)}) async-start(f32[8,1,1024]{2,1,0:T(1,128)} %get-tuple-element.27), calls=%async_computation.7 | async-start | bytes 65536 | tf_op jit(solution)/shard_map/all_to_all | solution.py:280
  126.9 4.7 %copy-start.2 = (f32[4096]{0:T(1024)S(1)}, f32[4096]{0:T(1024)}, u32[]{:S(2)}) copy-start(f32[4096]{0:T(1024)} %param.9) | copy-start | bytes 49156
Sparse Core Ops, SparseCore 0:
  10.8 51.8 reduce-scatter.1
  71.7 37.4 all-gather.1

commit v10 on v9

--- a/solution.py
+++ b/solution.py
@@ -305,9 +305,9 @@
     grad, row_new, packed = sums_of(pieces, aside, row_state[:, None], nmp)
     packed = fold(exchange(packed, NEAR), nz)
     packed = fold(exchange(packed, "z"), ny)
-    packed, state_sum = split_fold(exchange(packed, "y"), nmp)
+    packed, grad_input = lax.optimization_barrier((exchange(packed, "y"), grad_input))
+    packed, state_sum = split_fold(packed, nmp)
     packed = exchange(packed, NEAR).reshape(2 * cols // LANES, LANES)
-    packed, grad_input = lax.optimization_barrier((packed, grad_input))
     update, col_new, update_rms = update_of(
         packed, state_sum, grad, row_new, col_state.reshape(cols // LANES, LANES), entries
     )

time: 140 us -> 140 us (level)
  no operation moved by 1% of the time
where the time goes in v10:
time: 140 us; the launch traced here: 139 us
  blocking collectives  81.3 us (58%)
  waiting for transfers between devices  18.5 us (13%)
  between operations  14.2 us (10%)
  starting transfers between devices  13 us (9%)
  Pallas kernels  7.18 us (5%)
  matrix products  3.08 us (2%)
  local copies, waits for them, and re-layouts  1.45 us (1%)
    all_to_all x4, blocking collectives, exchange(): return lax.all_to_all(value, axes, 0, 0, tiled=True)  81.3 us
    all_to_all x3, waiting for transfers between devices, exchange(): return lax.all_to_all(value, axes, 0, 0, tiled=True)  18.5 us
    all_to_all x3, starting transfers between devices, exchange(): return lax.all_to_all(value, axes, 0, 0, tiled=True)  12.9 us
    pallas_call x1, Pallas kernels, term_of(): pl.pallas_call(functools.partial(term_kernel, inv_tokens), out_shape=jax....  3.44 us
    dot_general x1, matrix products, on_device(): lax.dot_general(cotangent, weight, (((1,), (1,)), ((), ())), preferred_el...  3.08 us
  transfers between devices with their start and end apart: 5, of which 3 were waited for; matrix products, arithmetic and copies ran while one was open for 3% of the time, Pallas kernels for 2%

profile of v10, /device:TPU:1, one launch (start us, length us, event | category | flops | bytes accessed | tf_op | source)
XLA Modules:
  0.0 139.3 jit_solution(7308330490608970637)
XLA Ops:
  7.2 0.0 reduce-scatter.2.cloned.1.call-start
  7.2 3.4 %term.1 = f32[64,8,1536]{2,1,0:T(8,128)} custom-call(bf16[192,256]{1,0:T(8,128)(2,1)} %context_ref, bf16[192,4096]{1,0:T(8,128)(2,1)} %cotangent_hbm.1), custom_call_target="tpu_custom_call" | custom-call | flops 402653184 | bytes 5767168 | tf_op jit(solution)/shard_map/term/pallas_call | solution.py:68
  10.7 0.0 copy-start.3
  10.7 0.0 copy-start
  10.7 0.0 copy-start.1
  10.7 0.0 reduce-scatter.2.cloned.1.call-update
  10.7 0.0 all-gather.2.cloned.1.call-start
  10.8 1.3 copy-done.3
  12.1 0.0 copy-done
  12.1 0.0 copy-done.1
  12.1 0.6 aside.1
  12.7 43.5 %all_to_all.35.value_ref = bf16[8,8,16,640]{3,2,1,0:T(8,128)(2,1)S(1)} all-to-all(bf16[8,8,16,640]{3,2,1,0:T(8,128)(2,1)S(1)} %aside.1), channel_id=1, replica_groups=mesh['y'=8,'z'=8,'x'=4,'c'=2] {'z'}, dimensions={0} | all-to-all | bytes 2621440 | tf_op jit(solution)/shard_map/all_to_all | solution.py:280
  56.2 0.7 arrival.1
  57.0 14.5 %all_to_all.36.aside_ref = f32[8,8,512]{2,1,0:T(8,128)S(1)} all-to-all(f32[8,8,512]{2,1,0:T(8,128)S(1)} %get-tuple-element.23), channel_id=1, replica_groups=mesh['y'=8,'z'=8,'x'=4,'c'=2] {'y'}, dimensions={0} | all-to-all | bytes 262144 | tf_op jit(solution)/shard_map/all_to_all | solution.py:280
  71.5 0.0 all-gather.2.cloned.1.call-update
  71.5 3.5 %all-to-all-start.2 = ((f32[8,8,1536]{2,1,0:T(8,128)}), f32[8,8,1536]{2,1,0:T(8,128)S(1)}, u32[]{:S(2)}, u32[]{:S(2)}) async-start(f32[8,8,1536]{2,1,0:T(8,128)} %bitcast.14), calls=%async_computation.3 | async-start | bytes 786432 | tf_op jit(solution)/shard_map/all_to_all | solution.py:280
  75.0 0.1 copy.11.state_ref
  75.1 10.6 %all-to-all-done.2.pieces_ref = f32[8,8,1536]{2,1,0:T(8,128)S(1)} async-done(((f32[8,8,1536]{2,1,0:T(8,128)}), f32[8,8,1536]{2,1,0:T(8,128)S(1)}, u32[]{:S(2)}, u32[]{:S(2)}) %all-to-all-start.2) | async-done | bytes 393248 | tf_op jit(solution)/shard_map/all_to_all | solution.py:280
  85.8 0.2 sums.1
  86.0 13.9 %all_to_all.37.value_ref = f32[8,1,1152]{2,1,0:T(1,128)S(1)} all-to-all(f32[8,1,1152]{2,1,0:T(1,128)S(1)} %get-tuple-element.26), channel_id=1, replica_groups=mesh['y'=8,'z'=8,'x'=4,'c'=2] {'x','c'}, dimensions={0} | all-to-all | bytes 73728 | tf_op jit(solution)/shard_map/all_to_all | solution.py:280
  99.9 9.4 %all_to_all.38.value_ref = f32[8,1,1152]{2,1,0:T(1,128)S(1)} all-to-all(f32[8,1,1152]{2,1,0:T(1,128)S(1)} %fold.2), channel_id=1, replica_groups=mesh['y'=8,'z'=8,'x'=4,'c'=2] {'z'}, dimensions={0} | all-to-all | bytes 73728 | tf_op jit(solution)/shard_map/all_to_all | solution.py:280
  109.3 0.6 fold.3
  109.9 3.3 %all-to-all-start.5 = ((f32[8,1,1152]{2,1,0:T(1,128)}), f32[8,1,1152]{2,1,0:T(1,128)S(1)}, u32[]{:S(2)}, u32[]{:S(2)}) async-start(f32[8,1,1152]{2,1,0:T(1,128)} %fold.3), calls=%async_computation.6 | async-start | bytes 73728 | tf_op jit(solution)/shard_map/all_to_all | solution.py:280
  113.3 0.0 copy-start.2
  113.3 0.0 all-gather.2.cloned.1.call-done
  113.3 3.1 %fusion = bf16[192,256]{1,0:T(8,128)(2,1)} fusion(bf16[256,4096]{1,0:T(8,128)(2,1)} %all-gather.2.cloned.1.call-done, bf16[192,4096]{1,0:T(8,128)(2,1)S(1)} %copy-done.3), kind=kOutput, calls=%fused_computation.1 | convolution fusion | flops 402702336 | bytes 3768320 | tf_op jit(solution)/shard_map/dot_general | solution.py:300
  116.4 3.7 %all-to-all-done.5.value_ref = f32[8,1,1152]{2,1,0:T(1,128)S(1)} async-done(((f32[8,1,1152]{2,1,0:T(1,128)}), f32[8,1,1152]{2,1,0:T(1,128)S(1)}, u32[]{:S(2)}, u32[]{:S(2)}) %all-to-all-start.5) | async-done | bytes 36896 | tf_op jit(solution)/shard_map/all_to_all | solution.py:280
  120.1 0.6 split_fold.1
  120.8 6.1 %all-to-all-start.6 = ((f32[8,1,1024]{2,1,0:T(1,128)}), f32[8,1,1024]{2,1,0:T(1,128)S(1)}, u32[]{:S(2)}, u32[]{:S(2)}) async-start(f32[8,1,1024]{2,1,0:T(1,128)} %get-tuple-element.30), calls=%async_computation.7 | async-start | bytes 65536 | tf_op jit(solution)/shard_map/all_to_all | solution.py:280
  126.9 0.6 reduce
  127.5 4.1 %all-to-all-done.6 = f32[8,1,1024]{2,1,0:T(1,128)S(1)} async-done(((f32[8,1,1024]{2,1,0:T(1,128)}), f32[8,1,1024]{2,1,0:T(1,128)S(1)}, u32[]{:S(2)}, u32[]{:S(2)}) %all-to-all-start.6) | async-done | bytes 32800 | tf_op jit(solution)/shard_map/all_to_all | solution.py:280
  131.6 0.9 update.1
  (6 shorter events, 0.1 us)
Async XLA Ops:
  7.2 64.4 %reduce-scatter.2.cloned.1.call-start = ((), (), s32[]{:S(2)}) async-start(), calls=%async_computation.8 | async-start | bytes 3538944 | tf_op jit(solution)/shard_map/reduce_scatter | solution.py:291
  10.7 1.4 %copy-start.3 = (bf16[192,4096]{1,0:T(8,128)(2,1)S(1)}, bf16[192,4096]{1,0:T(8,128)(2,1)}, u32[]{:S(2)}) copy-start(bf16[192,4096]{1,0:T(8,128)(2,1)} %cotangent_hbm.1) | copy-start | bytes 4718596
  10.7 1.4 %copy-start = (bf16[192,256]{1,0:T(8,128)(2,1)S(1)}, bf16[192,256]{1,0:T(8,128)(2,1)}, u32[]{:S(2)}) copy-start(bf16[192,256]{1,0:T(8,128)(2,1)} %context_ref) | copy-start | bytes 294916
  10.7 1.4 %copy-start.1 = (f32[4,4096]{1,0:T(4,128)S(1)}, f32[4,4096]{1,0:T(4,128)}, u32[]{:S(2)}) copy-start(f32[4,4096]{1,0:T(4,128)} %weight_ref.1) | copy-start | bytes 196612
  10.7 102.6 %all-gather.2.cloned.1.call-start = ((), (), s32[]{:S(2)}) async-start(), calls=%async_computation.9 | async-start | bytes 2359296 | tf_op jit(solution)/shard_map/all_gather | solution.py:299
  56.2 18.8 %copy-start.4 = (f32[4]{0:T(128)S(1)}, f32[4]{0:T(128)}, u32[]{:S(2)}) copy-start(f32[4]{0:T(128)} %param.8) | copy-start | bytes 52
  71.5 14.2 %all-to-all-start.2 = ((f32[8,8,1536]{2,1,0:T(8,128)}), f32[8,8,1536]{2,1,0:T(8,128)S(1)}, u32[]{:S(2)}, u32[]{:S(2)}) async-start(f32[8,8,1536]{2,1,0:T(8,128)} %bitcast.14), calls=%async_computation.3 | async-start | bytes 786432 | tf_op jit(solution)/shard_map/all_to_all | solution.py:280
  109.9 10.2 %all-to-all-start.5 = ((f32[8,1,1152]{2,1,0:T(1,128)}), f32[8,1,1152]{2,1,0:T(1,128)S(1)}, u32[]{:S(2)}, u32[]{:S(2)}) async-start(f32[8,1,1152]{2,1,0:T(1,128)} %fold.3), calls=%async_computation.6 | async-start | bytes 73728 | tf_op jit(solution)/shard_map/all_to_all | solution.py:280
  113.3 18.4 %copy-start.2 = (f32[4096]{0:T(1024)S(1)}, f32[4096]{0:T(1024)}, u32[]{:S(2)}) copy-start(f32[4096]{0:T(1024)} %param.9) | copy-start | bytes 49156
  120.8 10.9 %all-to-all-start.6 = ((f32[8,1,1024]{2,1,0:T(1,128)}), f32[8,1,1024]{2,1,0:T(1,128)S(1)}, u32[]{:S(2)}, u32[]{:S(2)}) async-start(f32[8,1,1024]{2,1,0:T(1,128)} %get-tuple-element.30), calls=%async_computation.7 | async-start | bytes 65536 | tf_op jit(solution)/shard_map/all_to_all | solution.py:280
Sparse Core Ops, SparseCore 0:
  10.8 51.8 reduce-scatter.1
  71.7 37.4 all-gather.1

commit v11 on v9

--- a/solution.py
+++ b/solution.py
@@ -14,6 +14,7 @@
 ASIDE = 512
 LANES = 128
 NEAR = ("x", "c")
+FAR = ("y", "z")
 VMEM = pl.BlockSpec(memory_space=pltpu.VMEM)
 PARAMS = pltpu.CompilerParams(vmem_limit_bytes=32 * 2**20)
 
@@ -303,9 +304,8 @@
 
     pieces = exchange(part.reshape(nz, 2 * rows, term.shape[2]), "z")
     grad, row_new, packed = sums_of(pieces, aside, row_state[:, None], nmp)
-    packed = fold(exchange(packed, NEAR), nz)
-    packed = fold(exchange(packed, "z"), ny)
-    packed, state_sum = split_fold(exchange(packed, "y"), nmp)
+    packed = fold(exchange(packed, NEAR), ny * nz)
+    packed, state_sum = split_fold(exchange(packed, FAR), nmp)
     packed = exchange(packed, NEAR).reshape(2 * cols // LANES, LANES)
     packed, grad_input = lax.optimization_barrier((packed, grad_input))
     update, col_new, update_rms = update_of(

time: 140 us -> 140 us (level)
  blocking collectives: 81.3 us -> 71.9 us
  waiting for transfers between devices: 18.5 us -> 26.3 us
  starting transfers between devices: 13 us -> 14.6 us
    all_to_all x4 -> x3, blocking collectives: 81.3 us -> 71.9 us  [exchange(): return lax.all_to_all(value, axes, 0, 0, tiled=True)]
    all_to_all x3, waiting for transfers between devices: 18.5 us -> 26.3 us  [exchange(): return lax.all_to_all(value, axes, 0, 0, tiled=True)]
    all_to_all x3, starting transfers between devices: 12.9 us -> 14.5 us  [exchange(): return lax.all_to_all(value, axes, 0, 0, tiled=True)]
where the time goes in v11:
time: 140 us
  blocking collectives  71.9 us (51%)
  waiting for transfers between devices  26.3 us (19%)
  starting transfers between devices  14.6 us (10%)
  between operations  14.1 us (10%)
  Pallas kernels  7.45 us (5%)
  matrix products  3.09 us (2%)
  local copies, waits for them, and re-layouts  1.44 us (1%)
    all_to_all x3, blocking collectives, exchange(): return lax.all_to_all(value, axes, 0, 0, tiled=True)  71.9 us
    all_to_all x3, waiting for transfers between devices, exchange(): return lax.all_to_all(value, axes, 0, 0, tiled=True)  26.3 us
    all_to_all x3, starting transfers between devices, exchange(): return lax.all_to_all(value, axes, 0, 0, tiled=True)  14.5 us
    pallas_call x1, Pallas kernels, term_of(): pl.pallas_call(functools.partial(term_kernel, inv_tokens), out_shape=jax....  3.44 us
    dot_general x1, matrix products, on_device(): lax.dot_general(cotangent, weight, (((1,), (1,)), ((), ())), preferred_el...  3.09 us
  transfers between devices with their start and end apart: 5, of which 3 were waited for; matrix products, arithmetic and copies ran while one was open for 3% of the time, Pallas kernels for 2%

profile of v11, /device:TPU:1, one launch (start us, length us, event | category | flops | bytes accessed | tf_op | source)
XLA Modules:
  0.0 139.6 jit_solution(5206942694602884223)
XLA Ops:
  7.2 0.0 reduce-scatter.2.cloned.1.call-start
  7.2 3.4 %term.1 = f32[64,8,1536]{2,1,0:T(8,128)} custom-call(bf16[192,256]{1,0:T(8,128)(2,1)} %context_ref, bf16[192,4096]{1,0:T(8,128)(2,1)} %cotangent_hbm.1), custom_call_target="tpu_custom_call" | custom-call | flops 402653184 | bytes 5767168 | tf_op jit(solution)/shard_map/term/pallas_call | solution.py:69
  10.7 0.0 copy-start.3
  10.7 0.0 copy-start
  10.7 0.0 copy-start.1
  10.7 0.0 reduce-scatter.2.cloned.1.call-update
  10.7 0.0 all-gather.2.cloned.1.call-start
  10.8 1.3 copy-done.3
  12.1 0.0 copy-done
  12.1 0.0 copy-done.1
  12.1 0.6 aside.1
  12.7 43.5 %all_to_all.30.value_ref = bf16[8,8,16,640]{3,2,1,0:T(8,128)(2,1)S(1)} all-to-all(bf16[8,8,16,640]{3,2,1,0:T(8,128)(2,1)S(1)} %aside.1), channel_id=1, replica_groups=mesh['y'=8,'z'=8,'x'=4,'c'=2] {'z'}, dimensions={0} | all-to-all | bytes 2621440 | tf_op jit(solution)/shard_map/all_to_all | solution.py:281
  56.2 0.0 copy-start.4
  56.2 0.7 arrival.1
  57.0 14.5 %all_to_all.31.aside_ref = f32[8,8,512]{2,1,0:T(8,128)S(1)} all-to-all(f32[8,8,512]{2,1,0:T(8,128)S(1)} %get-tuple-element.23), channel_id=1, replica_groups=mesh['y'=8,'z'=8,'x'=4,'c'=2] {'y'}, dimensions={0} | all-to-all | bytes 262144 | tf_op jit(solution)/shard_map/all_to_all | solution.py:281
  71.5 0.0 all-gather.2.cloned.1.call-update
  71.5 3.5 %all-to-all-start.2 = ((f32[8,8,1536]{2,1,0:T(8,128)}), f32[8,8,1536]{2,1,0:T(8,128)S(1)}, u32[]{:S(2)}, u32[]{:S(2)}) async-start(f32[8,8,1536]{2,1,0:T(8,128)} %bitcast.14), calls=%async_computation.3 | async-start | bytes 786432 | tf_op jit(solution)/shard_map/all_to_all | solution.py:281
  75.0 0.0 copy-done.4
  75.0 0.1 copy.11.state_ref
  75.1 10.6 %all-to-all-done.2.pieces_ref = f32[8,8,1536]{2,1,0:T(8,128)S(1)} async-done(((f32[8,8,1536]{2,1,0:T(8,128)}), f32[8,8,1536]{2,1,0:T(8,128)S(1)}, u32[]{:S(2)}, u32[]{:S(2)}) %all-to-all-start.2) | async-done | bytes 393248 | tf_op jit(solution)/shard_map/all_to_all | solution.py:281
  85.8 0.2 sums.1
  86.0 13.9 %all_to_all.32.value_ref = f32[8,1,1152]{2,1,0:T(1,128)S(1)} all-to-all(f32[8,1,1152]{2,1,0:T(1,128)S(1)} %get-tuple-element.26), channel_id=1, replica_groups=mesh['y'=8,'z'=8,'x'=4,'c'=2] {'x','c'}, dimensions={0} | all-to-all | bytes 73728 | tf_op jit(solution)/shard_map/all_to_all | solution.py:281
  99.9 0.8 fold.1
  100.6 4.6 %all-to-all-start.4 = ((f32[64,1,1152]{2,1,0:T(1,128)}), f32[64,1,1152]{2,1,0:T(1,128)S(1)}, u32[]{:S(2)}, u32[]{:S(2)}) async-start(f32[64,1,1152]{2,1,0:T(1,128)} %fold.1), calls=%async_computation.5 | async-start | bytes 589824 | tf_op jit(solution)/shard_map/all_to_all | solution.py:281
  105.3 0.6 reduce
  105.9 14.0 %all-to-all-done.4.value_ref = f32[64,1,1152]{2,1,0:T(1,128)S(1)} async-done(((f32[64,1,1152]{2,1,0:T(1,128)}), f32[64,1,1152]{2,1,0:T(1,128)S(1)}, u32[]{:S(2)}, u32[]{:S(2)}) %all-to-all-start.4) | async-done | bytes 294944 | tf_op jit(solution)/shard_map/all_to_all | solution.py:281
  119.9 0.8 split_fold.1
  120.7 6.5 %all-to-all-start.5 = ((f32[8,1,1024]{2,1,0:T(1,128)}), f32[8,1,1024]{2,1,0:T(1,128)S(1)}, u32[]{:S(2)}, u32[]{:S(2)}) async-start(f32[8,1,1024]{2,1,0:T(1,128)} %get-tuple-element.27), calls=%async_computation.6 | async-start | bytes 65536 | tf_op jit(solution)/shard_map/all_to_all | solution.py:281
  127.2 3.1 %fusion = bf16[192,256]{1,0:T(8,128)(2,1)} fusion(bf16[256,4096]{1,0:T(8,128)(2,1)} %all-gather.2.cloned.1.call-done, bf16[192,4096]{1,0:T(8,128)(2,1)S(1)} %copy-done.3), kind=kOutput, calls=%fused_computation.1 | convolution fusion | flops 402702336 | bytes 3768320 | tf_op jit(solution)/shard_map/dot_general | solution.py:301
  130.3 1.6 %all-to-all-done.5 = f32[8,1,1024]{2,1,0:T(1,128)S(1)} async-done(((f32[8,1,1024]{2,1,0:T(1,128)}), f32[8,1,1024]{2,1,0:T(1,128)S(1)}, u32[]{:S(2)}, u32[]{:S(2)}) %all-to-all-start.5) | async-done | bytes 32800 | tf_op jit(solution)/shard_map/all_to_all | solution.py:281
  131.9 0.0 copy-done.2
  131.9 0.9 update.1
  (4 shorter events, 0.0 us)
Async XLA Ops:
  7.2 64.4 %reduce-scatter.2.cloned.1.call-start = ((), (), s32[]{:S(2)}) async-start(), calls=%async_computation.7 | async-start | bytes 3538944 | tf_op jit(solution)/shard_map/reduce_scatter | solution.py:292
  10.7 1.4 %copy-start.3 = (bf16[192,4096]{1,0:T(8,128)(2,1)S(1)}, bf16[192,4096]{1,0:T(8,128)(2,1)}, u32[]{:S(2)}) copy-start(bf16[192,4096]{1,0:T(8,128)(2,1)} %cotangent_hbm.1) | copy-start | bytes 4718596
  10.7 1.4 %copy-start = (bf16[192,256]{1,0:T(8,128)(2,1)S(1)}, bf16[192,256]{1,0:T(8,128)(2,1)}, u32[]{:S(2)}) copy-start(bf16[192,256]{1,0:T(8,128)(2,1)} %context_ref) | copy-start | bytes 294916
  10.7 1.4 %copy-start.1 = (f32[4,4096]{1,0:T(4,128)S(1)}, f32[4,4096]{1,0:T(4,128)}, u32[]{:S(2)}) copy-start(f32[4,4096]{1,0:T(4,128)} %weight_ref.1) | copy-start | bytes 196612
  10.7 116.4 %all-gather.2.cloned.1.call-start = ((), (), s32[]{:S(2)}) async-start(), calls=%async_computation.8 | async-start | bytes 2359296 | tf_op jit(solution)/shard_map/all_gather | solution.py:300
  56.2 18.8 %copy-start.4 = (f32[4]{0:T(128)S(1)}, f32[4]{0:T(128)}, u32[]{:S(2)}) copy-start(f32[4]{0:T(128)} %param.8) | copy-start | bytes 52
  71.5 14.2 %all-to-all-start.2 = ((f32[8,8,1536]{2,1,0:T(8,128)}), f32[8,8,1536]{2,1,0:T(8,128)S(1)}, u32[]{:S(2)}, u32[]{:S(2)}) async-start(f32[8,8,1536]{2,1,0:T(8,128)} %bitcast.14), calls=%async_computation.3 | async-start | bytes 786432 | tf_op jit(solution)/shard_map/all_to_all | solution.py:281
  100.6 19.3 %all-to-all-start.4 = ((f32[64,1,1152]{2,1,0:T(1,128)}), f32[64,1,1152]{2,1,0:T(1,128)S(1)}, u32[]{:S(2)}, u32[]{:S(2)}) async-start(f32[64,1,1152]{2,1,0:T(1,128)} %fold.1), calls=%async_computation.5 | async-start | bytes 589824 | tf_op jit(solution)/shard_map/all_to_all | solution.py:281
  120.7 11.2 %all-to-all-start.5 = ((f32[8,1,1024]{2,1,0:T(1,128)}), f32[8,1,1024]{2,1,0:T(1,128)S(1)}, u32[]{:S(2)}, u32[]{:S(2)}) async-start(f32[8,1,1024]{2,1,0:T(1,128)} %get-tuple-element.27), calls=%async_computation.6 | async-start | bytes 65536 | tf_op jit(solution)/shard_map/all_to_all | solution.py:281
  127.2 4.7 %copy-start.2 = (f32[4096]{0:T(1024)S(1)}, f32[4096]{0:T(1024)}, u32[]{:S(2)}) copy-start(f32[4096]{0:T(1024)} %param.9) | copy-start | bytes 49156
Sparse Core Ops, SparseCore 0:
  10.8 51.8 reduce-scatter.1
  71.7 39.6 all-gather.1
